TPU v7x, 128 devices: a whole 4x4x4 slice. The times are simulated.
128 devices in a mesh: role: 2 (over core), batch: 8 (over x_lo, z), tensor: 8 (over y, x_hi).
Axes of the slice: x: 4 (x_hi: 2, x_lo: 2; x = x_hi * 2 + x_lo), y: 4, z: 4, core: 2. Of those that a mesh axis runs over, the one named last changes fastest.
Arguments:
- span_x: bfloat16 [8192, 8192], P('batch'), may hold values from -40 to 40
- norm_gain: bfloat16 [8192], replicated, may hold values from 0.099609375 to 1.8984375
- key_value_weight: bfloat16 [8192, 8, 2, 128], P(None, 'tensor', 'role'), may hold values from -0.0625 to 0.0625
- key_value_bias: bfloat16 [8, 2, 128], P('tensor', 'role'), may hold values from -4 to 4
- queries: bfloat16 [4, 256, 64, 128], P(None, ('role', 'batch'), 'tensor'), may hold values from -200 to 200
- decode_key_value: bfloat16 [4, 256, 8, 2, 128], P(None, ('role', 'batch'), 'tensor'), may hold values from -4 to 4
- kv_cache: bfloat16 [256, 256, 8, 2, 128], P(('role', 'batch'), None, 'tensor'), may hold values from -4 to 4
- w_out: bfloat16 [8192, 8192], P('tensor', ('role', 'batch')), may hold values from -0.5 to 0.5
- members: int32 [256], replicated, may hold values from 0 to 255, as said below
- span_req: int32 [8192], replicated, may hold values from 0 to 255, as said below
- span_pos: int32 [8192], replicated, may hold values from 2 to 767, as said below
- cache_len: int32 [256], replicated, may hold values from 2 to 256, as said below
Outputs:
- layer_output: bfloat16 [256, 4, 8192], P('tensor', None, ('role', 'batch'))
Inputs may be any that keep to these rules, and one draw needn't show every extreme that they name: `members`: A permutation: each request sits in exactly one decode slot; decode owner o holds slots o * 16 to o * 16 + 15. `span_req`: in every block of 1024 consecutive span tokens, exactly 64 tokens belong to the requests of each decode owner. `span_pos`: the span tokens of request r take, in span order, the positions cache_len[r], cache_len[r] + 1, and so on. `cache_len`: some request has exactly 256 cached tokens.
All inputs are finite; a program needn't handle non-finite values.
Results may differ from a plain program's by a relative error of at most 0.017.
Values may be sent and summed in bfloat16 or wider, within the bound.
No kernel may reach another device: no remote copies, remote signals or barrier semaphores. Data moves between devices by JAX's collectives and lax.ppermute only.
A program may use at most 128 MiB of HBM per device.

v0:
```python
import math

import jax
import jax.numpy as jnp
from jax import lax
from jax.sharding import PartitionSpec as P

EPSILON = 1e-06
THETA_BASE = 1000000.0
NEGATIVE = -1e30


def rms_normed(span_x, norm_gain):
    as_float = span_x.astype(jnp.float32)
    square_mean = jnp.mean(as_float * as_float, axis=-1, keepdims=True)
    return (as_float * lax.rsqrt(square_mean + EPSILON) * norm_gain.astype(jnp.float32)).astype(
        jnp.bfloat16
    )


def rotate_keys(values_in, positions):
    half_dim = values_in.shape[-1] // 2
    inv_freq = THETA_BASE ** (-jnp.arange(half_dim, dtype=jnp.float32) / half_dim)
    angles = positions.astype(jnp.float32)[:, None] * inv_freq[None, :]
    cosine = jnp.cos(angles)[:, None, :]
    sine_part = jnp.sin(angles)[:, None, :]
    first_half = values_in[..., :half_dim]
    second_half = values_in[..., half_dim:]
    return jnp.concatenate(
        [
            first_half * cosine - second_half * sine_part,
            second_half * cosine + first_half * sine_part,
        ],
        axis=-1,
    )


def body(
    span_x,
    norm_gain,
    key_value_weight,
    key_value_bias,
    queries,
    decode_key_value,
    kv_cache,
    w_out,
    members,
    span_req,
    span_pos,
    cache_len,
):
    n_role = lax.axis_size("role")
    n_batch = lax.axis_size("batch")
    owners = n_role * n_batch
    my_role = lax.axis_index("role")
    my_batch = lax.axis_index("batch")
    my_owner = my_role * n_batch + my_batch
    sub_rows = span_x.shape[0]
    capacity = sub_rows // owners
    width = span_x.shape[1]
    kv_heads = key_value_weight.shape[1]
    head_dim = key_value_weight.shape[3]
    steps_count = queries.shape[0]
    slot_count = queries.shape[1]
    heads_per_group = queries.shape[2] // kv_heads
    requests = members.shape[0]
    span_rows = span_req.shape[0]
    features = kv_heads * head_dim
    normalized_input = rms_normed(span_x, norm_gain)
    projected_rows = jnp.dot(
        normalized_input,
        key_value_weight.reshape(width, features),
        preferred_element_type=jnp.float32,
    )
    projected_rows = (
        projected_rows + key_value_bias.reshape(features).astype(jnp.float32)
    ).reshape(sub_rows, kv_heads, head_dim)
    my_positions = lax.dynamic_slice_in_dim(span_pos, my_batch * sub_rows, sub_rows)
    rotated = rotate_keys(projected_rows, my_positions)
    outgoing = (
        jnp.where(my_role == 0, rotated, projected_rows)
        .astype(jnp.bfloat16)
        .reshape(sub_rows, features)
    )
    request_ids = jnp.arange(requests, dtype=jnp.int32)
    slot_owner = request_ids // slot_count
    owner_of_request = jnp.sum(
        jnp.where(members[None, :] == request_ids[:, None], slot_owner[None, :], 0), axis=1
    )
    token_owner = jnp.sum(
        jnp.where(span_req[:, None] == request_ids[None, :], owner_of_request[None, :], 0), axis=1
    )
    blocks = span_rows // sub_rows
    block_owner = token_owner.reshape(blocks, sub_rows)
    mine_first = jnp.argsort((block_owner != my_owner).astype(jnp.int32), axis=1, stable=True)[
        :, :capacity
    ]
    chosen = (mine_first + jnp.arange(blocks, dtype=jnp.int32)[:, None] * sub_rows).reshape(-1)
    row_request = span_req[chosen]
    everything = lax.all_gather(outgoing, ("role", "batch"), axis=0, tiled=True)
    key_rows = everything[:span_rows][chosen]
    value_rows = everything[span_rows:][chosen]
    span_keys = key_rows.reshape(-1, kv_heads, head_dim)
    span_values = value_rows.reshape(-1, kv_heads, head_dim)
    scale = 1.0 / math.sqrt(head_dim)
    grouped_queries = queries.reshape(steps_count, slot_count, kv_heads, heads_per_group, head_dim)
    my_members = lax.dynamic_slice_in_dim(members, my_owner * slot_count, slot_count)
    my_lengths = jnp.sum(
        jnp.where(my_members[:, None] == request_ids[None, :], cache_len[None, :], 0), axis=1
    )
    cache_mask = jnp.arange(kv_cache.shape[1], dtype=jnp.int32)[None, :] < my_lengths[:, None]
    span_mask = row_request[None, :] == my_members[:, None]
    step_ids = jnp.arange(steps_count, dtype=jnp.int32)
    fresh_mask = step_ids[None, :] <= step_ids[:, None]
    cache_mask = cache_mask[None, :, None, None, :]
    span_mask = span_mask[None, :, None, None, :]
    fresh_mask = fresh_mask[:, None, None, None, :]
    cache_scores = (
        jnp.einsum(
            "jsgmd,spgd->jsgmp",
            grouped_queries,
            kv_cache[:, :, :, 0, :],
            preferred_element_type=jnp.float32,
        )
        * scale
    )
    span_scores = (
        jnp.einsum(
            "jsgmd,rgd->jsgmr", grouped_queries, span_keys, preferred_element_type=jnp.float32
        )
        * scale
    )
    fresh_scores = (
        jnp.einsum(
            "jsgmd,isgd->jsgmi",
            grouped_queries,
            decode_key_value[:, :, :, 0, :],
            preferred_element_type=jnp.float32,
        )
        * scale
    )
    cache_scores = jnp.where(cache_mask, cache_scores, NEGATIVE)
    span_scores = jnp.where(span_mask, span_scores, NEGATIVE)
    fresh_scores = jnp.where(fresh_mask, fresh_scores, NEGATIVE)
    top = jnp.maximum(
        jnp.maximum(
            jnp.max(cache_scores, axis=-1, keepdims=True),
            jnp.max(span_scores, axis=-1, keepdims=True),
        ),
        jnp.max(fresh_scores, axis=-1, keepdims=True),
    )
    cache_exp = jnp.where(cache_mask, jnp.exp(cache_scores - top), 0.0)
    span_exp = jnp.where(span_mask, jnp.exp(span_scores - top), 0.0)
    fresh_exp = jnp.where(fresh_mask, jnp.exp(fresh_scores - top), 0.0)
    total = (
        jnp.sum(cache_exp, axis=-1, keepdims=True)
        + jnp.sum(span_exp, axis=-1, keepdims=True)
        + jnp.sum(fresh_exp, axis=-1, keepdims=True)
    )
    cache_weights = (cache_exp / total).astype(jnp.bfloat16)
    span_weights = (span_exp / total).astype(jnp.bfloat16)
    fresh_weights = (fresh_exp / total).astype(jnp.bfloat16)
    mixed = jnp.einsum(
        "jsgmp,spgd->jsgmd",
        cache_weights,
        kv_cache[:, :, :, 1, :],
        preferred_element_type=jnp.float32,
    )
    mixed = mixed + jnp.einsum(
        "jsgmr,rgd->jsgmd", span_weights, span_values, preferred_element_type=jnp.float32
    )
    mixed = mixed + jnp.einsum(
        "jsgmi,isgd->jsgmd",
        fresh_weights,
        decode_key_value[:, :, :, 1, :],
        preferred_element_type=jnp.float32,
    )
    attention = mixed.astype(jnp.bfloat16)
    head_rows = attention.transpose(1, 0, 2, 3, 4).reshape(
        slot_count, steps_count, kv_heads * heads_per_group * head_dim
    )
    gathered = lax.all_gather(head_rows, ("role", "batch"), axis=0, tiled=True)
    return lax.psum_scatter(
        jnp.einsum("rjc,cn->rjn", gathered, w_out, preferred_element_type=jnp.float32).astype(
            jnp.bfloat16
        ),
        "tensor",
        scatter_dimension=0,
        tiled=True,
    )


def solution(mesh):
    placed = (
        P("batch", None),
        P(),
        P(None, "tensor", "role", None),
        P("tensor", "role", None),
        P(None, ("role", "batch"), "tensor", None),
        P(None, ("role", "batch"), "tensor", None, None),
        P(("role", "batch"), None, "tensor", None, None),
        P("tensor", ("role", "batch")),
        P(),
        P(),
        P(),
        P(),
    )
    return jax.shard_map(
        body,
        mesh=mesh,
        in_specs=placed,
        out_specs=P("tensor", None, ("role", "batch")),
        check_vma=False,
    )
```

profile of v0, /device:TPU:0, one launch (start us, length us, event | category | flops | bytes accessed | tf_op | source)
XLA Modules:
  0.0 222.4 jit_solution(388667999709111208)
XLA Ops:
  7.4 0.9 select_reduce_fusion.1
  8.3 3.3 %select_reduce_fusion = s32[8192]{0:T(1024)S(1)} fusion(s32[256]{0:T(256)S(1)} %select_reduce_fusion.1, s32[8192]{0:T(1024)} %param.21), kind=kLoop, calls=%fused_computation.11 | loop fusion | flops 6283264 | bytes 66560 | tf_op jit(solution)/shard_map/reduce_sum | solution.py:90
  13.7 7.2 %fusion = f32[1024]{0:T(1024)S(1)} fusion(bf16[1024,8192]{1,0:T(8,128)(2,1)} %param.12), kind=kLoop, calls=%fused_computation.5 | loop fusion | flops 25164800 | bytes 16781312 | tf_op jit(solution)/shard_map/reduce_sum | solution.py:15
  21.7 9.6 %fusion.11 = f32[1024,128]{0,1:T(8,128)S(1)} fusion(bf16[8192,1,1,128]{3,0,2,1:T(8,128)(2,1)S(1)} %copy-done, bf16[1024,8192]{1,0:T(8,128)(2,1)} %param.12, f32[8192]{0:T(1024)S(1)} %convert_element_type.51, f32[1024]{0:T(1024)S(1)} %add_rsqrt_fusion, f32[128]{0:T(128)S(1)} %bitcast_convert_fusion), kind=kOutput, calls=%fused_computation.20 | convolution fusion | flops 2181169152 | bytes 19436032 | tf_op jit(solution)/shard_map/dot_general | solution.py:70
  31.3 1.2 fusion.34
  34.4 1.3 fusion.56
  35.7 6.5 %fusion.54 = (bf16[16,256,1,1,128]{4,3,2,1,0:T(2,128)(2,1)}, bf16[16,256,1,1,128]{4,3,2,1,0:T(2,128)(2,1)S(1)}) fusion(bf16[16,256,1,2,128]{4,3,2,1,0:T(2,128)(2,1)} %param.18), kind=kLoop, calls=%fused_computation.98 | loop fusion | bytes 4194304 | tf_op jit(solution)/shard_map/slice | solution.py:166
  42.2 1.9 fusion.57
  45.0 3.1 %gather_fusion = s32[512]{0:T(512)S(1)} fusion(s32[8192]{0:T(1024)S(1)} %copy-done.1, s32[1024]{0:T(1024)S(1)} %pad_clamp_fusion), kind=kCustom, calls=%fused_computation | custom fusion | bytes 6144 | tf_op jit(solution)/shard_map/gather | solution.py:99
  48.2 25.5 %all-gather.3.cloned.1.call-done = bf16[16384,128]{0,1:T(8,128)(2,1)} async-done(((bf16[1024,128]{0,1:T(8,128)(2,1)}), bf16[16384,128]{0,1:T(8,128)(2,1)}) %all-gather.3.cloned.1.call-update) | async-done | bytes 4194320 | tf_op jit(solution)/shard_map/all_gather | solution.py:100
  73.7 4.7 %fusion.53 = (bf16[8192,128]{0,1:T(8,128)(2,1)}, bf16[8192,128]{0,1:T(8,128)(2,1)}) fusion(bf16[16384,128]{0,1:T(8,128)(2,1)} %all-gather.3.cloned.1.call-done), kind=kLoop, calls=%fused_computation.97 | loop fusion | bytes 8388608 | tf_op jit(solution)/shard_map/slice | solution.py:102
  78.4 4.1 %copy.75 = bf16[8192,128]{1,0:T(8,128)(2,1)} copy(bf16[8192,128]{0,1:T(8,128)(2,1)} %get-tuple-element.8) | data formatting | bytes 4194304 | tf_op jit(solution)/shard_map/slice | solution.py:101
  82.5 2.9 %gather_fusion.1 = bf16[512,128]{1,0:T(8,128)(2,1)S(1)} fusion(bf16[8192,128]{1,0:T(8,128)(2,1)} %copy.75, s32[1024]{0:T(1024)S(1)} %pad_clamp_fusion), kind=kCustom, calls=%fused_computation.1 | custom fusion | bytes 264192 | tf_op jit(solution)/shard_map/gather | solution.py:101
  85.4 1.0 fusion.58
  86.4 0.8 copy.77
  88.5 1.3 fusion.28
  90.7 1.1 fusion.27
  91.8 2.8 %convolution_bitcast_fusion.1 = f32[16,4,1,8,128]{4,3,1,0,2:T(8,128)} fusion(bf16[16,256,1,1,128]{4,3,2,1,0:T(2,128)(2,1)} %get-tuple-element.9, f32[4,16,1,8,256]{4,3,0,1,2:T(8,128)} %get-tuple-element.18, f32[4,16,8]{2,0,1:T(4,128)S(1)} %bitcast.130, f32[4,16,8]{2,0,1:T(4,128)S(1)} %bitcast.126, pred[16,256]{1,0:T(8,128)(4,1)S(1)} %iota_compare_fusion.3), kind=kOutput, calls=%fused_computation.26 | convolution fusion | flops 34078720 | bytes 1843200 | tf_op jit(solution)/shard_map/jsgmp,spgd->jsgmd/dot_general | solution.py:163
  94.9 4.2 %copy.83 = bf16[8192,128]{1,0:T(8,128)(2,1)} copy(bf16[8192,128]{0,1:T(8,128)(2,1)} %get-tuple-element.7) | data formatting | bytes 4194304 | tf_op jit(solution)/shard_map/slice | solution.py:102
  99.1 2.9 %gather_fusion.2 = bf16[512,128]{1,0:T(8,128)(2,1)S(1)} fusion(bf16[8192,128]{1,0:T(8,128)(2,1)} %copy.83, s32[1024]{0:T(1024)S(1)} %pad_clamp_fusion), kind=kCustom, calls=%fused_computation.2 | custom fusion | bytes 264192 | tf_op jit(solution)/shard_map/gather | solution.py:102
  103.3 34.2 %all-gather.5.cloned.1.call-done = bf16[256,4,1024]{2,0,1:T(8,128)(2,1)} async-done(((bf16[16,4,1024]{2,0,1:T(8,128)(2,1)}), bf16[256,4,1024]{2,0,1:T(8,128)(2,1)}) %all-gather.5.cloned.1.call-update) | async-done | bytes 2097168 | tf_op jit(solution)/shard_map/all_gather | solution.py:182
  137.5 4.1 %convolution_convert_fusion = bf16[256,4,512]{2,0,1:T(8,128)(2,1)} fusion(bf16[256,4,1024]{2,0,1:T(8,128)(2,1)} %all-gather.5.cloned.1.call-done, bf16[1024,512]{1,0:T(8,128)(2,1)} %param.19), kind=kOutput, calls=%fused_computation.14 | convolution fusion | flops 1074266112 | bytes 4194304 | tf_op jit(solution)/shard_map/rjc,cn->rjn/dot_general | solution.py:184
  141.6 71.7 %reduce-scatter.2.cloned.1.call-done = bf16[32,4,512]{2,0,1:T(8,128)(2,1)} async-done(((bf16[256,4,512]{2,0,1:T(8,128)(2,1)}), bf16[32,4,512]{2,0,1:T(8,128)(2,1)}) %reduce-scatter.2.cloned.1.call-update) | async-done | bytes 131088 | tf_op jit(solution)/shard_map/reduce_scatter | solution.py:183
  213.4 1.7 copy.88
  (65 shorter events, 9.3 us)
Async XLA Ops:
  7.4 14.3 %copy-start = (bf16[8192,1,1,128]{3,0,2,1:T(8,128)(2,1)S(1)}, bf16[8192,1,1,128]{3,0,2,1:T(8,128)(2,1)}, u32[]{:S(2)}) copy-start(bf16[8192,1,1,128]{3,0,2,1:T(8,128)(2,1)} %param.14) | copy-start | bytes 6291460
  7.4 36.8 %sort.19.cloned.1.call-start = ((), (), s32[]{:S(2)}) async-start(), calls=%async_computation.4 | async-start | bytes 196640 | tf_op jit(solution)/shard_map/jit(argsort)/sort | solution.py:95
  12.9 60.8 %all-gather.3.cloned.1.call-start = ((), (), s32[]{:S(2)}) async-start(), calls=%async_computation.1 | async-start | bytes 4456448 | tf_op jit(solution)/shard_map/all_gather | solution.py:100
  13.7 7.2 %copy-start.10 = (bf16[1,1,128]{2,1,0:T(2,128)(2,1)S(1)}, bf16[1,1,128]{2,1,0:T(2,128)(2,1)}, u32[]{:S(2)}) copy-start(bf16[1,1,128]{2,1,0:T(2,128)(2,1)} %param.15) | copy-start | bytes 772
  31.3 2.1 copy-start.6
  31.3 2.2 copy-start.7
  31.3 2.4 %copy-start.3 = (bf16[4,16,1,2,128]{4,3,2,1,0:T(2,128)(2,1)S(1)}, bf16[4,16,1,2,128]{4,3,2,1,0:T(2,128)(2,1)}, u32[]{:S(2)}) copy-start(bf16[4,16,1,2,128]{4,3,2,1,0:T(2,128)(2,1)} %param.17) | copy-start | bytes 98308
  31.3 3.1 %copy-start.4 = (bf16[4,16,8,128]{3,2,1,0:T(8,128)(2,1)S(1)}, bf16[4,16,8,128]{3,2,1,0:T(8,128)(2,1)}, u32[]{:S(2)}) copy-start(bf16[4,16,8,128]{3,2,1,0:T(8,128)(2,1)} %param.16) | copy-start | bytes 393220
  33.3 104.2 %all-gather.5.cloned.1.call-start = ((), (), s32[]{:S(2)}) async-start(), calls=%async_computation.2 | async-start | bytes 2228224 | tf_op jit(solution)/shard_map/all_gather | solution.py:182
  33.5 8.8 %copy-start.8 = (pred[4,4]{1,0:T(4,128)(4,1)}, pred[4,4]{1,0:T(4,128)(4,1)S(1)}, u32[]{:S(2)}) copy-start(pred[4,4]{1,0:T(4,128)(4,1)S(1)} %iota_compare_fusion.4) | copy-start | bytes 52
  42.2 2.8 %copy-start.1 = (s32[8192]{0:T(1024)S(1)}, s32[8192]{0:T(1024)}, u32[]{:S(2)}) copy-start(s32[8192]{0:T(1024)} %param.21) | copy-start | bytes 98308
  91.8 2.8 %copy-start.5 = (bf16[4,16,1,1,128]{4,3,2,1,0:T(2,128)(2,1)S(1)}, bf16[4,16,1,1,128]{4,3,2,1,0:T(2,128)(2,1)}, u32[]{:S(2)}) copy-start(bf16[4,16,1,1,128]{4,3,2,1,0:T(2,128)(2,1)} %get-tuple-element.13) | copy-start | bytes 49156
  91.8 2.8 %copy-start.9 = (pred[4,4]{1,0:T(4,128)(4,1)S(1)}, pred[4,4]{1,0:T(4,128)(4,1)}, u32[]{:S(2)}) copy-start(pred[4,4]{1,0:T(4,128)(4,1)} %copy-done.8) | copy-start | bytes 52
  94.9 7.1 %copy-start.2 = (bf16[4,16,8,512]{3,1,2,0:T(8,128)(2,1)S(1)}, bf16[4,16,8,512]{3,1,2,0:T(8,128)(2,1)}, u32[]{:S(2)}) copy-start(bf16[4,16,8,512]{3,1,2,0:T(8,128)(2,1)} %fusion.27) | copy-start | bytes 1572868
  94.9 7.1 %copy-start.11 = (f32[16,4,1,8,128]{4,3,1,0,2:T(8,128)S(1)}, f32[16,4,1,8,128]{4,3,1,0,2:T(8,128)}, u32[]{:S(2)}) copy-start(f32[16,4,1,8,128]{4,3,1,0,2:T(8,128)} %convolution_bitcast_fusion.1) | copy-start | bytes 786436
  103.3 110.1 %reduce-scatter.2.cloned.1.call-start = ((), (), s32[]{:S(2)}) async-start(), calls=%async_computation.3 | async-start | bytes 1179648 | tf_op jit(solution)/shard_map/reduce_scatter | solution.py:183
Sparse Core Ops, SparseCore 0:
  13.0 3.0 sort.21.cloned.1.call-done
  141.7 71.5 reduce-scatter.1
  (1 shorter events, 0.0 us)
Sparse Core Ops, SparseCore 1:
  33.4 40.2 all-gather.2
  103.4 34.1 all-gather.4
where the time goes:
time: 223 us; the launch traced here: 222 us
  waiting for transfers between devices  131 us (59%)
  local copies, waits for them, and re-layouts  34 us (15%)
  matrix products  21.5 us (10%)
  other arithmetic  20.3 us (9%)
  between operations  15.1 us (7%)
    reduce_scatter x1, waiting for transfers between devices, body(): lax.psum_scatter(jnp.einsum('rjc,cn->rjn', gathered, w_out, preferred_ele...  71.7 us
    all_gather x1, waiting for transfers between devices, body(): gathered = lax.all_gather(head_rows, ('role', 'batch'), axis=0, tiled=True)  34.2 us
    all_gather x1, waiting for transfers between devices, body(): everything = lax.all_gather(outgoing, ('role', 'batch'), axis=0, tiled=True)  25.5 us
    dot_general x1, matrix products, body(): jnp.dot(normalized_input, key_value_weight.reshape(width, features), pref...  9.62 us
    slice x2, local copies, waits for them, and re-layouts, body(): value_rows = everything[span_rows:][chosen]  8.87 us
    reduce_sum x1, other arithmetic, rms_normed(): square_mean = jnp.mean(as_float * as_float, axis=-1, keepdims=True)  7.22 us
    slice x1, local copies, waits for them, and re-layouts, body(): kv_cache[:, :, :, 1, :]  6.52 us
  transfers between devices with their start and end apart: 3, of which 3 were waited for; matrix products, arithmetic and copies ran while one was open for 7% of the time, Pallas kernels for 0%

commit v1 on v0

v1 whole, which is shorter than its diff:
```python
import functools
import math

import jax
import jax.numpy as jnp
import numpy as np
from jax import lax
from jax.experimental import pallas as pl
from jax.experimental.pallas import tpu as pltpu
from jax.sharding import PartitionSpec as P

EPSILON = 1e-06
THETA_BASE = 1000000.0
NEGATIVE = -1e30
F32 = jnp.float32
BF16 = jnp.bfloat16
MIB = 1024 * 1024


def nt_dot(a, b):
    return lax.dot_general(a, b, (((1,), (1,)), ((), ())), preferred_element_type=F32)


def nn_dot(a, b):
    return jnp.dot(a, b, preferred_element_type=F32)


def iota(shape, dim):
    return lax.broadcasted_iota(jnp.int32, shape, dim)


def as_mask(cond, dtype=BF16):
    return jnp.where(cond, 1.0, 0.0).astype(dtype)


def to_column(rows):
    eye = as_mask(iota((128, 128), 0) == iota((128, 128), 1))
    return nt_dot(eye, rows.astype(BF16))


def prefill_kernel(
    place,
    x_ref,
    gain_ref,
    weight_ref,
    bias_ref,
    freq_ref,
    request_ref,
    position_ref,
    member_ref,
    out_ref,
    acc_ref,
    square_ref,
    cos_ref,
    sin_ref,
    perm_ref,
    ids_ref,
    carry_ref,
    column_ref,
    poscol_ref,
):
    step = pl.program_id(0)
    steps = pl.num_programs(0)
    rows = x_ref.shape[0]
    width = x_ref.shape[1] * steps
    owners = out_ref.shape[0]
    capacity = rows // owners
    groups = rows // 128
    slots = member_ref.shape[0] * 128
    per_owner = slots // owners

    @pl.when(step == 0)
    def _():
        acc_ref[...] = jnp.zeros_like(acc_ref)
        square_ref[...] = jnp.zeros_like(square_ref)
        ids_ref[...] = jnp.zeros_like(ids_ref)
        carry_ref[...] = jnp.zeros_like(carry_ref)
        members = member_ref[...]
        filler = jnp.zeros((8 - members.shape[0], 128), jnp.int32)
        turned = to_column(jnp.concatenate([members, filler], axis=0).astype(F32))
        for part in range(slots // 128):
            column_ref[part * 128 : (part + 1) * 128, :] = jnp.broadcast_to(
                turned[:, part : part + 1], (128, 128)
            )
        positions = jnp.where(place[0] == 0, position_ref[...], 0)
        high = to_column((positions // 32).astype(F32))
        low = to_column((positions % 32).astype(F32))
        turned = high * 32.0 + low
        for part in range(groups):
            poscol_ref[part] = jnp.broadcast_to(turned[:, part : part + 1], (128, 128))

    lane = iota((128, 128), 1)
    angles = poscol_ref[step] * freq_ref[...]
    quarter = jnp.floor(angles * (2.0 / math.pi) + 0.5)
    rest = angles - quarter * 1.5703125
    rest = rest - quarter * 4.837512969970703125e-4
    rest = rest - quarter * 7.54978995489188216e-8
    square = rest * rest
    sine = rest + rest * square * (
        -1.6666654611e-1 + square * (8.3321608736e-3 + square * -1.9515295891e-4)
    )
    cosine = (
        1.0
        - 0.5 * square
        + square
        * square
        * (4.166664568298827e-2 + square * (-1.388731625493765e-3 + square * 2.443315711809948e-5))
    )
    turn = quarter.astype(jnp.int32) + jnp.where(lane < 64, 1, 0)
    table = jnp.where((turn & 1) == 1, cosine, sine)
    table = jnp.where((turn & 2) == 2, -table, table)
    swapped = pltpu.roll(table, 64, axis=1)
    cos_ref[step] = jnp.where(lane < 64, table, swapped)
    sin_ref[step] = jnp.where(lane < 64, -swapped, table)

    request_row = request_ref[pl.ds(step, 1), :].astype(F32)
    held = as_mask(column_ref[...] == request_row)
    pick_row = iota((32, slots), 0)
    pick_slot = iota((32, slots), 1)
    pick = jnp.where(pick_row == 16, pick_slot % per_owner, 0)
    pick = jnp.where((pick_row < 16) & (pick_slot // per_owner == pick_row), 1, pick)
    found = nn_dot(pick.astype(F32).astype(BF16), held)
    owner_hot = found[:16]
    slot_row = found[16:24]
    hot = owner_hot.astype(BF16)
    before = nn_dot(hot, as_mask(iota((128, 128), 0) < iota((128, 128), 1)))
    ranks = before + carry_ref[...] + (iota((16, 128), 0) * capacity).astype(F32)
    carry_ref[...] += nn_dot(hot, jnp.ones((128, 128), BF16))
    target = jnp.sum(owner_hot * ranks, axis=0, keepdims=True).astype(jnp.int32)
    chosen = as_mask(iota((rows, 128), 0) == target)
    perm_ref[step] = chosen
    ids_ref[...] += nt_dot(slot_row.astype(BF16), chosen)

    chunk = min(rows, 256)

    def project(index, _):
        start = pl.multiple_of(index * chunk, chunk)
        strips = []
        for strip in range(chunk // 16):
            block = x_ref[pl.ds(start + strip * 16, 16), :]
            strips.append(block * gain_ref[...])
            wide = block.astype(F32)
            wide = wide * wide
            total = wide[:, :128]
            for tile in range(1, wide.shape[1] // 128):
                total = total + wide[:, tile * 128 : (tile + 1) * 128]
            square_ref[pl.ds(start + strip * 16, 16), :] += total
        acc_ref[pl.ds(start, chunk), :] += nn_dot(
            jnp.concatenate(strips, axis=0), weight_ref[...]
        )
        return 0

    lax.fori_loop(0, rows // chunk, project, 0)

    @pl.when(step == steps - 1)
    def _():
        mean = jnp.sum(square_ref[...], axis=1, keepdims=True) / width
        scaled = acc_ref[...] * lax.rsqrt(mean + EPSILON) + bias_ref[...].astype(F32)
        cosines = cos_ref[...].reshape(rows, 128)
        sines = sin_ref[...].reshape(rows, 128)
        rotated = scaled * cosines + pltpu.roll(scaled, 64, axis=1) * sines
        rounded = rotated.astype(BF16)
        everything = jnp.concatenate([perm_ref[part] for part in range(groups)], axis=1)
        ordered = nn_dot(everything, rounded).astype(BF16)
        lanes = iota((16, 128), 1)
        for owner in range(owners):
            out_ref[owner, :capacity, :] = ordered[owner * capacity : (owner + 1) * capacity]
            pair = owner // 2
            ids = jnp.broadcast_to(ids_ref[0:1, pair * 128 : (pair + 1) * 128], (16, 128))
            other = pltpu.roll(ids, 64, axis=1)
            mine = (lanes < 64) if owner % 2 == 0 else (lanes >= 64)
            out_ref[owner, capacity:, :] = jnp.where(mine, ids, other).astype(BF16)


def prefill(place, span_x, norm_gain, weight, bias, span_req, span_pos, members, owners):
    rows, width = span_x.shape
    head_dim = weight.shape[1]
    groups = rows // 128
    tile = width // groups
    half = head_dim // 2
    freq = (THETA_BASE ** (-(np.arange(head_dim) % half) / half)).astype(np.float32)[None, :]
    whole = lambda *shape: pl.BlockSpec(shape, lambda k, place: (0,) * len(shape))
    mine = pl.BlockSpec((groups, 128), lambda k, place: (place[1], 0))
    return pl.pallas_call(
        prefill_kernel,
        out_shape=jax.ShapeDtypeStruct((owners, rows // owners + 16, head_dim), BF16),
        grid_spec=pltpu.PrefetchScalarGridSpec(
            num_scalar_prefetch=1,
            grid=(groups,),
            in_specs=[
                pl.BlockSpec((rows, tile), lambda k, place: (0, k)),
                pl.BlockSpec((1, tile), lambda k, place: (0, k)),
                pl.BlockSpec((tile, head_dim), lambda k, place: (k, 0)),
                whole(1, head_dim),
                whole(1, head_dim),
                mine,
                mine,
                whole(members.shape[0] // 128, 128),
            ],
            out_specs=whole(owners, rows // owners + 16, head_dim),
            scratch_shapes=[
                pltpu.VMEM((rows, 128), F32),
                pltpu.VMEM((rows, 128), F32),
                pltpu.VMEM((groups, 128, 128), F32),
                pltpu.VMEM((groups, 128, 128), F32),
                pltpu.VMEM((groups, rows, 128), BF16),
                pltpu.VMEM((8, rows), F32),
                pltpu.VMEM((16, 128), F32),
                pltpu.VMEM((members.shape[0], 128), F32),
                pltpu.VMEM((groups, 128, 128), F32),
            ],
        ),
        compiler_params=pltpu.CompilerParams(
            dimension_semantics=("arbitrary",), vmem_limit_bytes=48 * MIB
        ),
        cost_estimate=pl.CostEstimate(
            flops=2 * rows * width * head_dim, bytes_accessed=2 * rows * width, transcendentals=0
        ),
        name="prefill",
    )(
        place,
        span_x,
        norm_gain.reshape(1, width),
        weight,
        bias,
        jnp.asarray(freq),
        span_req.reshape(-1, 128),
        span_pos.reshape(-1, 128),
        members.reshape(-1, 128),
    )


def attention_kernel(
    lengths, query_ref, cache_ref, fresh_ref, row_ref, out_ref, q_ref, s_ref, p_ref, sum_ref, acc_ref
):
    steps, slots, heads, dim = query_ref.shape
    per_slot = steps * heads
    rows = slots * per_slot
    cached = cache_ref.shape[1]
    blocks = row_ref.shape[0] // 2
    capacity = row_ref.shape[1] - 16
    spanned = blocks * capacity
    newest = fresh_ref.shape[0]
    scale = 1.0 / math.sqrt(dim)
    for slot in range(slots):
        q_ref[slot * per_slot : (slot + 1) * per_slot, :] = jnp.concatenate(
            [query_ref[step, slot].astype(F32) for step in range(steps)], axis=0
        ).astype(BF16)
    column = iota((per_slot, cached), 1)
    for slot in range(slots):
        span = pl.ds(slot * per_slot, per_slot)
        scores = nt_dot(q_ref[span, :], cache_ref[slot]) * scale
        keep = ((column & 1) == 0) & (column < 2 * lengths[slot])
        s_ref[span, :cached] = jnp.where(keep, scores, NEGATIVE)
    keys = [row_ref[block, :capacity, :] for block in range(blocks)]
    values = [row_ref[blocks + block, :capacity, :] for block in range(blocks)]
    lane = iota((16, 128), 1)
    row_slot = iota((rows, 128), 0) // per_slot
    for pair in range(spanned // 128):
        scores = nt_dot(q_ref[...], jnp.concatenate(keys[2 * pair : 2 * pair + 2], axis=0)) * scale
        left = row_ref[2 * pair, capacity:, :].astype(F32)
        right = row_ref[2 * pair + 1, capacity:, :].astype(F32)
        ids = jnp.where(lane < 64, left, right)[0:1].astype(jnp.int32)
        s_ref[:, cached + pair * 128 : cached + (pair + 1) * 128] = jnp.where(
            row_slot == ids, scores, NEGATIVE
        )
    row = iota((rows, newest), 0)
    col = iota((rows, newest), 1)
    per_step = 2 * slots
    keep = (
        ((col & 1) == 0)
        & ((col % per_step) // 2 == row // per_slot)
        & (col // per_step <= (row % per_slot) // heads)
    )
    scores = nt_dot(q_ref[...], fresh_ref[...]) * scale
    s_ref[:, cached + spanned :] = jnp.where(keep, scores, NEGATIVE)
    for slot in range(slots):
        span = pl.ds(slot * per_slot, per_slot)
        scores = s_ref[span, :]
        top = jnp.max(scores, axis=1, keepdims=True)
        weights = jnp.exp(scores - top)
        sum_ref[span, :] = jnp.broadcast_to(jnp.sum(weights, axis=1, keepdims=True), (per_slot, dim))
        p_ref[span, :cached] = pltpu.roll(weights[:, :cached], 1, axis=1).astype(BF16)
        p_ref[span, cached : cached + spanned] = weights[:, cached : cached + spanned].astype(BF16)
        p_ref[span, cached + spanned :] = pltpu.roll(
            weights[:, cached + spanned :], 1, axis=1
        ).astype(BF16)
    acc_ref[...] = nn_dot(
        p_ref[:, cached : cached + spanned], jnp.concatenate(values, axis=0)
    ) + nn_dot(p_ref[:, cached + spanned :], fresh_ref[...])
    for slot in range(slots):
        span = pl.ds(slot * per_slot, per_slot)
        acc_ref[span, :] = (
            acc_ref[span, :] + nn_dot(p_ref[span, :cached], cache_ref[slot])
        ) / sum_ref[span, :]
    for head in range(heads):
        out_ref[head] = acc_ref[pl.ds(head, slots * steps, stride=heads), :].astype(BF16)


def attend(lengths, queries, cache, fresh, rows):
    steps, slots, heads, dim = queries.shape
    count = slots * steps * heads
    cached = cache.shape[1]
    spanned = (rows.shape[0] // 2) * (rows.shape[1] - 16)
    columns = cached + spanned + fresh.shape[0]
    vmem = pl.BlockSpec(memory_space=pltpu.VMEM)
    return pl.pallas_call(
        attention_kernel,
        out_shape=jax.ShapeDtypeStruct((heads, slots * steps, dim), BF16),
        in_specs=[pl.BlockSpec(memory_space=pltpu.SMEM)] + [vmem] * 4,
        out_specs=vmem,
        scratch_shapes=[
            pltpu.VMEM((count, dim), BF16),
            pltpu.VMEM((count, columns), F32),
            pltpu.VMEM((count, columns), BF16),
            pltpu.VMEM((count, dim), F32),
            pltpu.VMEM((count, dim), F32),
        ],
        compiler_params=pltpu.CompilerParams(vmem_limit_bytes=32 * MIB),
        name="attend",
    )(lengths, queries, cache, fresh, rows)


def body(
    span_x,
    norm_gain,
    key_value_weight,
    key_value_bias,
    queries,
    decode_key_value,
    kv_cache,
    w_out,
    members,
    span_req,
    span_pos,
    cache_len,
):
    n_role = lax.axis_size("role")
    n_batch = lax.axis_size("batch")
    owners = n_role * n_batch
    my_role = lax.axis_index("role")
    my_batch = lax.axis_index("batch")
    my_owner = my_role * n_batch + my_batch
    width = span_x.shape[1]
    head_dim = key_value_weight.shape[3]
    steps, slots, heads, _ = queries.shape
    place = jnp.stack([my_role, my_batch]).astype(jnp.int32)
    outgoing = prefill(
        place,
        span_x,
        norm_gain,
        key_value_weight.reshape(width, head_dim),
        key_value_bias.reshape(1, head_dim),
        span_req,
        span_pos,
        members,
        owners,
    )
    arrived = lax.all_to_all(outgoing, ("role", "batch"), 0, 0)
    my_members = lax.dynamic_slice_in_dim(members, my_owner * slots, slots)
    request_ids = jnp.arange(members.shape[0], dtype=jnp.int32)
    lengths = jnp.sum(
        jnp.where(my_members[:, None] == request_ids[None, :], cache_len[None, :], 0), axis=1
    )
    attention = attend(
        lengths,
        queries,
        kv_cache.reshape(slots, -1, head_dim),
        decode_key_value.reshape(-1, head_dim),
        arrived,
    )

    def shifted(k):
        pairs = []
        for i in range(n_batch):
            pairs.append((i, (((i // 4) ^ (k // 4)) * 4) + (i % 4 + k % 4) % 4))
        return pairs

    blocks = [attention]
    for k in range(1, n_batch):
        blocks.append(lax.ppermute(attention, "batch", shifted(k)))
    mine = jnp.stack(blocks)
    other = lax.ppermute(mine, "role", [(0, 1), (1, 0)])

    def rows_of(stack):
        return stack.transpose(0, 2, 1, 3).reshape(n_batch, slots * steps, heads * head_dim)

    def product(stack):
        return jnp.einsum("brc,cn->brn", rows_of(stack), w_out, preferred_element_type=F32).astype(
            BF16
        )

    sender = jnp.array(
        [[[s for s, d in shifted(k) if d == i][0] for k in range(n_batch)] for i in range(n_batch)],
        jnp.int32,
    )[my_batch]
    slot_of = jnp.sum(
        jnp.where(sender[None, :] == jnp.arange(n_batch)[:, None], jnp.arange(n_batch)[None, :], 0),
        axis=1,
    )
    first = jnp.where(my_role == 0, mine, other)
    second = jnp.where(my_role == 0, other, mine)
    partial = jnp.concatenate([product(first)[slot_of], product(second)[slot_of]], axis=0)
    n_tensor = lax.axis_size("tensor")
    partial = partial.reshape(n_tensor, -1, w_out.shape[1])
    summed = jnp.sum(lax.all_to_all(partial, "tensor", 0, 0).astype(F32), axis=0).astype(BF16)
    return summed.reshape(-1, steps, w_out.shape[1])


def solution(mesh):
    placed = (
        P("batch", None),
        P(),
        P(None, "tensor", "role", None),
        P("tensor", "role", None),
        P(None, ("role", "batch"), "tensor", None),
        P(None, ("role", "batch"), "tensor", None, None),
        P(("role", "batch"), None, "tensor", None, None),
        P("tensor", ("role", "batch")),
        P(),
        P(),
        P(),
        P(),
    )
    return jax.shard_map(
        body,
        mesh=mesh,
        in_specs=placed,
        out_specs=P("tensor", None, ("role", "batch")),
        check_vma=False,
    )
```

time: 223 us -> 94.1 us (0.42)
  waiting for transfers between devices: 131 us -> 23.9 us
  blocking collectives: 0 us -> 23.9 us
  local copies, waits for them, and re-layouts: 34 us -> 10.3 us
  Pallas kernels: 0 us -> 20.6 us
  matrix products: 21.5 us -> 1.41 us
  other arithmetic: 20.3 us -> 0.77 us
  between operations: 15.1 us -> 0.22 us
  starting transfers between devices: 0.14 us -> 12.4 us
    reduce_scatter x1 -> x0, waiting for transfers between devices: 71.7 us -> none  [body(): lax.psum_scatter(jnp.einsum('rjc,cn->rjn', gathered, w_out, preferred_ele...]
    all_gather x2 -> x0, waiting for transfers between devices: 59.6 us -> none  [the longest x1 34.2 us: body(): gathered = lax.all_gather(head_rows, ('role', 'batch'), axis=0, tiled=True)]
    all_to_all x0 -> x1, blocking collectives: none -> 23.9 us  [body(): lax.all_to_all(partial, 'tensor', 0, 0).astype(F32)]
    pallas_call x0 -> x2, Pallas kernels: none -> 20.6 us  [the longest x1 18 us: prefill(): pl.pallas_call(prefill_kernel, out_shape=jax.ShapeDtypeStruct((owners, ro...]
    slice x5 -> x0, local copies, waits for them, and re-layouts: 20.2 us -> none  [the longest x2 8.87 us: body(): value_rows = everything[span_rows:][chosen]]
    dot_general x8 -> x2, matrix products: 21.5 us -> 1.41 us  [product(): jnp.einsum('brc,cn->brn', rows_of(stack), w_out, preferred_element_type=F32)]
    ppermute x0 -> x8, waiting for transfers between devices: none -> 15.6 us  [the longest x7 13.8 us: body(): blocks.append(lax.ppermute(attention, 'batch', shifted(k)))]
    reduce_sum x6 -> x2, other arithmetic: 13.9 us -> 0.27 us  [the longest x1 0.15 us: body(): jnp.sum(lax.all_to_all(partial, 'tensor', 0, 0).astype(F32), axis=0)]
  transfers between devices with their start and end apart: 3 -> 9, of which waited for: 3 -> 5; matrix products, arithmetic and copies ran while one was open for 7% -> 1% of each run, Pallas kernels for 0% -> 0%
where the time goes in v1:
time: 94.1 us; the launch traced here: 93.6 us
  waiting for transfers between devices  23.9 us (25%)
  blocking collectives  23.9 us (25%)
  Pallas kernels  20.6 us (22%)
  starting transfers between devices  12.4 us (13%)
  local copies, waits for them, and re-layouts  10.3 us (11%)
  matrix products  1.41 us (1%)
    all_to_all x1, blocking collectives, body(): lax.all_to_all(partial, 'tensor', 0, 0).astype(F32)  23.9 us
    pallas_call x1, Pallas kernels, prefill(): pl.pallas_call(prefill_kernel, out_shape=jax.ShapeDtypeStruct((owners, ro...  18 us
    ppermute x7, waiting for transfers between devices, body(): blocks.append(lax.ppermute(attention, 'batch', shifted(k)))  13.8 us
    all_to_all x1, waiting for transfers between devices, body(): arrived = lax.all_to_all(outgoing, ('role', 'batch'), 0, 0)  8.28 us
    unnamed x33, local copies, waits for them, and re-layouts  6.85 us
    all_to_all x1, starting transfers between devices, body(): arrived = lax.all_to_all(outgoing, ('role', 'batch'), 0, 0)  6.4 us
    ppermute x7, starting transfers between devices, body(): blocks.append(lax.ppermute(attention, 'batch', shifted(k)))  5.92 us
    pallas_call x1, Pallas kernels, attend(): pl.pallas_call(attention_kernel, out_shape=jax.ShapeDtypeStruct((heads, s...  2.62 us
  transfers between devices with their start and end apart: 9, of which 5 were waited for; matrix products, arithmetic and copies ran while one was open for 1% of the time, Pallas kernels for 0%

profile of v1, /device:TPU:0, one launch (start us, length us, event | category | flops | bytes accessed | tf_op | source)
XLA Modules:
  0.0 93.6 jit_solution(11879024919618291512)
XLA Ops:
  0.0 0.8 reshape.53.gain_ref
  0.9 1.6 %copy-done.1 = bf16[8192,1,1,128]{3,0,2,1:T(8,128)(2,1)S(1)} copy-done((bf16[8192,1,1,128]{3,0,2,1:T(8,128)(2,1)S(1)}, bf16[8192,1,1,128]{3,0,2,1:T(8,128)(2,1)}, u32[]{:S(2)}) %copy-start.1) | copy-done | bytes 2097176
  2.5 0.8 copy-done.5
  3.3 0.8 copy-done.6
  4.0 0.7 copy-done.8
  5.4 0.7 copy-done.11
  6.0 18.0 %prefill.1 = bf16[16,80,128]{2,1,0:T(8,128)(2,1)S(1)} custom-call(s32[2]{0:T(128)S(1)} %pad_add_fusion.place, bf16[1024,8192]{1,0:T(8,128)(2,1)} %x_ref.1, bf16[1,8192]{1,0:T(2,128)(2,1)S(1)} %reshape.53.gain_ref, bf16[8192,128]{1,0:T(8,128)(2,1)S(1)} %bitcast.49, bf16[1,128]{1,0:T(2,128)(2,1)S(1)} %bitcast.55, f32[1,128]{1,0:T(1,128)S(1)} %copy-done.11, ...), custom_call_target="tpu_custom_call" | custom-call | flops 2147483648 | bytes 16777216 | tf_op jit(solution)/shard_map/prefill/pallas_call | solution.py:184
  24.0 0.7 copy-done.3
  24.7 6.4 %all-to-all-start = ((bf16[16,80,128]{2,1,0:T(8,128)(2,1)}), bf16[16,80,128]{2,1,0:T(8,128)(2,1)S(1)}, u32[]{:S(2)}, u32[]{:S(2)}) async-start(bf16[16,80,128]{2,1,0:T(8,128)(2,1)} %copy-done.3), calls=%async_computation | async-start | bytes 655360 | tf_op jit(solution)/shard_map/all_to_all | solution.py:359
  31.4 8.3 %all-to-all-done.row_ref = bf16[16,80,128]{2,1,0:T(8,128)(2,1)S(1)} async-done(((bf16[16,80,128]{2,1,0:T(8,128)(2,1)}), bf16[16,80,128]{2,1,0:T(8,128)(2,1)S(1)}, u32[]{:S(2)}, u32[]{:S(2)}) %all-to-all-start) | async-done | bytes 327712 | tf_op jit(solution)/shard_map/all_to_all | solution.py:359
  39.7 0.9 copy-done.4
  40.6 2.6 %attend.1 = bf16[8,64,128]{2,1,0:T(8,128)(2,1)S(1)} custom-call(s32[16]{0:T(128)S(1)} %select_reduce_fusion.lengths, bf16[4,16,8,128]{3,2,1,0:T(8,128)(2,1)S(1)} %copy-done.4, bf16[16,512,128]{2,1,0:T(8,128)(2,1)S(1)} %bitcast.50, bf16[128,128]{1,0:T(8,128)(2,1)S(1)} %bitcast.53, bf16[16,80,128]{2,1,0:T(8,128)(2,1)S(1)} %all-to-all-done.row_ref), custom_call_target="tpu_custom_call" | custom-call | tf_op jit(solution)/shard_map/attend/pallas_call | solution.py:307
  43.8 1.7 %collective-permute-start.1 = (bf16[8,64,128]{2,1,0:T(8,128)(2,1)S(1)}, bf16[8,64,128]{2,1,0:T(8,128)(2,1)S(1)}, u32[]{:S(2)}, u32[]{:S(2)}) collective-permute-start(bf16[8,64,128]{2,1,0:T(8,128)(2,1)S(1)} %attend.1), channel_id=1, source_target_pairs={{0,16},{8,24},{16,0},{24,8},{32,48},{40,56},{48,32},{56,40},{1,17}... | collective-permute-start | bytes 393224 | tf_op jit(solution)/shard_map/ppermute | solution.py:381
  45.6 1.8 %collective-permute-start.2 = (bf16[8,64,128]{2,1,0:T(8,128)(2,1)S(1)}, bf16[8,64,128]{2,1,0:T(8,128)(2,1)S(1)}, u32[]{:S(2)}, u32[]{:S(2)}) collective-permute-start(bf16[8,64,128]{2,1,0:T(8,128)(2,1)S(1)} %attend.1), channel_id=1, source_target_pairs={{0,24},{8,0},{16,8},{24,16},{32,56},{40,32},{48,40},{56,48},{1,25}... | collective-permute-start | bytes 393224 | tf_op jit(solution)/shard_map/ppermute | solution.py:381
  47.7 1.3 %collective-permute-start.4 = (bf16[8,64,128]{2,1,0:T(8,128)(2,1)S(1)}, bf16[8,64,128]{2,1,0:T(8,128)(2,1)S(1)}, u32[]{:S(2)}, u32[]{:S(2)}) collective-permute-start(bf16[8,64,128]{2,1,0:T(8,128)(2,1)S(1)} %attend.1), channel_id=1, source_target_pairs={{0,40},{8,48},{16,56},{24,32},{32,8},{40,16},{48,24},{56,0},{1,41}... | collective-permute-start | bytes 393224 | tf_op jit(solution)/shard_map/ppermute | solution.py:381
  49.1 6.3 %collective-permute-done = bf16[8,64,128]{2,1,0:T(8,128)(2,1)S(1)} collective-permute-done((bf16[8,64,128]{2,1,0:T(8,128)(2,1)S(1)}, bf16[8,64,128]{2,1,0:T(8,128)(2,1)S(1)}, u32[]{:S(2)}, u32[]{:S(2)}) %collective-permute-start) | collective-permute-done | bytes 131104 | tf_op jit(solution)/shard_map/ppermute | solution.py:381
  55.6 0.7 collective-permute-done.4
  56.3 6.8 %collective-permute-done.5 = bf16[8,64,128]{2,1,0:T(8,128)(2,1)S(1)} collective-permute-done((bf16[8,64,128]{2,1,0:T(8,128)(2,1)S(1)}, bf16[8,64,128]{2,1,0:T(8,128)(2,1)S(1)}, u32[]{:S(2)}, u32[]{:S(2)}) %collective-permute-start.5) | collective-permute-done | bytes 131104 | tf_op jit(solution)/shard_map/ppermute | solution.py:381
  63.3 0.7 dynamic-slice_bitcast_fusion
  64.1 1.8 %collective-permute-done.7 = bf16[8,8,64,128]{3,2,1,0:T(8,128)(2,1)S(1)} collective-permute-done((bf16[8,8,64,128]{3,2,1,0:T(8,128)(2,1)S(1)}, bf16[8,8,64,128]{3,2,1,0:T(8,128)(2,1)S(1)}, u32[]{:S(2)}, u32[]{:S(2)}) %collective-permute-start.7) | collective-permute-done | bytes 1048608 | tf_op jit(solution)/shard_map/ppermute | solution.py:383
  66.1 0.7 convolution_convert_fusion.1
  66.8 0.7 convolution_convert_fusion
  68.8 23.9 %all_to_all.10 = bf16[8,128,512]{2,1,0:T(8,128)(2,1)S(1)} all-to-all(bf16[8,128,512]{2,1,0:T(8,128)(2,1)S(1)} %bitcast.56), channel_id=1, replica_groups=mesh['role'=2,'batch'=8,'tensor'=8] {'tensor'}, dimensions={0} | all-to-all | bytes 2097152 | tf_op jit(solution)/shard_map/all_to_all | solution.py:406
  92.9 0.7 reshape.62
  (47 shorter events, 4.0 us)
Async XLA Ops:
  0.0 66.1 %copy-start = (bf16[1024,512]{1,0:T(8,128)(2,1)S(1)}, bf16[1024,512]{1,0:T(8,128)(2,1)}, u32[]{:S(2)}) copy-start(bf16[1024,512]{1,0:T(8,128)(2,1)} %param.21) | copy-start | bytes 3145732
  0.9 1.6 %copy-start.1 = (bf16[8192,1,1,128]{3,0,2,1:T(8,128)(2,1)S(1)}, bf16[8192,1,1,128]{3,0,2,1:T(8,128)(2,1)}, u32[]{:S(2)}) copy-start(bf16[8192,1,1,128]{3,0,2,1:T(8,128)(2,1)} %param.16) | copy-start | bytes 6291460
  2.5 0.8 copy-start.5
  3.3 0.8 copy-start.6
  4.0 0.7 copy-start.8
  4.7 0.7 copy-start.10
  5.4 0.7 copy-start.11
  6.0 25.1 %copy-start.9 = (s32[256]{0:T(256)S(1)}, s32[256]{0:T(256)}, u32[]{:S(2)}) copy-start(s32[256]{0:T(256)} %param.22) | copy-start | bytes 3076
  6.0 25.2 %copy-start.12 = (s32[256]{0:T(256)S(1)}, s32[256]{0:T(256)}, u32[]{:S(2)}) copy-start(s32[256]{0:T(256)} %param.25) | copy-start | bytes 3076
  6.0 33.7 %copy-start.2 = (bf16[16,256,1,2,128]{4,3,2,1,0:T(2,128)(2,1)S(1)}, bf16[16,256,1,2,128]{4,3,2,1,0:T(2,128)(2,1)}, u32[]{:S(2)}) copy-start(bf16[16,256,1,2,128]{4,3,2,1,0:T(2,128)(2,1)} %param.20) | copy-start | bytes 6291460
  6.0 33.7 %copy-start.7 = (bf16[4,16,1,2,128]{4,3,2,1,0:T(2,128)(2,1)S(1)}, bf16[4,16,1,2,128]{4,3,2,1,0:T(2,128)(2,1)}, u32[]{:S(2)}) copy-start(bf16[4,16,1,2,128]{4,3,2,1,0:T(2,128)(2,1)} %param.19) | copy-start | bytes 98308
  24.0 0.7 copy-start.3
  24.7 15.0 %all-to-all-start = ((bf16[16,80,128]{2,1,0:T(8,128)(2,1)}), bf16[16,80,128]{2,1,0:T(8,128)(2,1)S(1)}, u32[]{:S(2)}, u32[]{:S(2)}) async-start(bf16[16,80,128]{2,1,0:T(8,128)(2,1)} %copy-done.3), calls=%async_computation | async-start | bytes 655360 | tf_op jit(solution)/shard_map/all_to_all | solution.py:359
  39.7 0.9 copy-start.4
  43.2 12.1 %collective-permute-start = (bf16[8,64,128]{2,1,0:T(8,128)(2,1)S(1)}, bf16[8,64,128]{2,1,0:T(8,128)(2,1)S(1)}, u32[]{:S(2)}, u32[]{:S(2)}) collective-permute-start(bf16[8,64,128]{2,1,0:T(8,128)(2,1)S(1)} %attend.1), channel_id=1, source_target_pairs={{0,8},{8,16},{16,24},{24,0},{32,40},{40,48},{48,56},{56,32},{1,9},... | collective-permute-start | bytes 393224 | tf_op jit(solution)/shard_map/ppermute | solution.py:381
  43.8 11.5 %collective-permute-start.1 = (bf16[8,64,128]{2,1,0:T(8,128)(2,1)S(1)}, bf16[8,64,128]{2,1,0:T(8,128)(2,1)S(1)}, u32[]{:S(2)}, u32[]{:S(2)}) collective-permute-start(bf16[8,64,128]{2,1,0:T(8,128)(2,1)S(1)} %attend.1), channel_id=1, source_target_pairs={{0,16},{8,24},{16,0},{24,8},{32,48},{40,56},{48,32},{56,40},{1,17}... | collective-permute-start | bytes 393224 | tf_op jit(solution)/shard_map/ppermute | solution.py:381
  45.6 9.9 %collective-permute-start.2 = (bf16[8,64,128]{2,1,0:T(8,128)(2,1)S(1)}, bf16[8,64,128]{2,1,0:T(8,128)(2,1)S(1)}, u32[]{:S(2)}, u32[]{:S(2)}) collective-permute-start(bf16[8,64,128]{2,1,0:T(8,128)(2,1)S(1)} %attend.1), channel_id=1, source_target_pairs={{0,24},{8,0},{16,8},{24,16},{32,56},{40,32},{48,40},{56,48},{1,25}... | collective-permute-start | bytes 393224 | tf_op jit(solution)/shard_map/ppermute | solution.py:381
  47.3 8.2 %collective-permute-start.3 = (bf16[8,64,128]{2,1,0:T(8,128)(2,1)S(1)}, bf16[8,64,128]{2,1,0:T(8,128)(2,1)S(1)}, u32[]{:S(2)}, u32[]{:S(2)}) collective-permute-start(bf16[8,64,128]{2,1,0:T(8,128)(2,1)S(1)} %attend.1), channel_id=1, source_target_pairs={{0,32},{8,40},{16,48},{24,56},{32,0},{40,8},{48,16},{56,24},{1,33}... | collective-permute-start | bytes 393224 | tf_op jit(solution)/shard_map/ppermute | solution.py:381
  47.7 8.5 %collective-permute-start.4 = (bf16[8,64,128]{2,1,0:T(8,128)(2,1)S(1)}, bf16[8,64,128]{2,1,0:T(8,128)(2,1)S(1)}, u32[]{:S(2)}, u32[]{:S(2)}) collective-permute-start(bf16[8,64,128]{2,1,0:T(8,128)(2,1)S(1)} %attend.1), channel_id=1, source_target_pairs={{0,40},{8,48},{16,56},{24,32},{32,8},{40,16},{48,24},{56,0},{1,41}... | collective-permute-start | bytes 393224 | tf_op jit(solution)/shard_map/ppermute | solution.py:381
  55.3 7.8 %collective-permute-start.5 = (bf16[8,64,128]{2,1,0:T(8,128)(2,1)S(1)}, bf16[8,64,128]{2,1,0:T(8,128)(2,1)S(1)}, u32[]{:S(2)}, u32[]{:S(2)}) collective-permute-start(bf16[8,64,128]{2,1,0:T(8,128)(2,1)S(1)} %attend.1), channel_id=1, source_target_pairs={{0,48},{8,56},{16,32},{24,40},{32,16},{40,24},{48,0},{56,8},{1,49}... | collective-permute-start | bytes 393224 | tf_op jit(solution)/shard_map/ppermute | solution.py:381
  55.4 7.8 %collective-permute-start.6 = (bf16[8,64,128]{2,1,0:T(8,128)(2,1)S(1)}, bf16[8,64,128]{2,1,0:T(8,128)(2,1)S(1)}, u32[]{:S(2)}, u32[]{:S(2)}) collective-permute-start(bf16[8,64,128]{2,1,0:T(8,128)(2,1)S(1)} %attend.1), channel_id=1, source_target_pairs={{0,56},{8,32},{16,40},{24,48},{32,24},{40,0},{48,8},{56,16},{1,57}... | collective-permute-start | bytes 393224 | tf_op jit(solution)/shard_map/ppermute | solution.py:381
  63.2 2.7 %collective-permute-start.7 = (bf16[8,8,64,128]{3,2,1,0:T(8,128)(2,1)S(1)}, bf16[8,8,64,128]{3,2,1,0:T(8,128)(2,1)S(1)}, u32[]{:S(2)}, u32[]{:S(2)}) collective-permute-start(bf16[8,8,64,128]{3,2,1,0:T(8,128)(2,1)S(1)} %bitcast_dynamic-update-slice_fusion), channel_id=1, source_target_pairs={{0,64},{64,0},{1,65},{65,1},{2,66},{66,2},{3,67},{67,3},{4,68},{68... | collective-permute-start | bytes 3145736 | tf_op jit(solution)/shard_map/ppermute | solution.py:383

commit v2 on v1

v2 whole, which is shorter than its diff:
```python
import functools
import math

import jax
import jax.numpy as jnp
import numpy as np
from jax import lax
from jax.experimental import pallas as pl
from jax.experimental.pallas import tpu as pltpu
from jax.sharding import PartitionSpec as P

EPSILON = 1e-06
THETA_BASE = 1000000.0
NEGATIVE = -1e30
F32 = jnp.float32
BF16 = jnp.bfloat16
MIB = 1024 * 1024


def nt_dot(a, b):
    return lax.dot_general(a, b, (((1,), (1,)), ((), ())), preferred_element_type=F32)


def nn_dot(a, b):
    return jnp.dot(a, b, preferred_element_type=F32)


def iota(shape, dim):
    return lax.broadcasted_iota(jnp.int32, shape, dim)


def as_mask(cond, dtype=BF16):
    return jnp.where(cond, 1.0, 0.0).astype(dtype)


def to_column(rows):
    eye = as_mask(iota((128, 128), 0) == iota((128, 128), 1))
    return nt_dot(eye, rows.astype(BF16))


def prefill_kernel(
    place,
    x_hbm,
    weight_hbm,
    gain_hbm,
    bias_hbm,
    freq_hbm,
    request_hbm,
    position_hbm,
    member_hbm,
    out_ref,
    x_ref,
    weight_ref,
    gain_ref,
    bias_ref,
    freq_ref,
    request_ref,
    position_ref,
    member_ref,
    spread_ref,
    perm_ref,
    rounded_ref,
    x_sem,
    weight_sem,
    small_sem,
):
    rows, width = x_hbm.shape
    depth = x_ref.shape[0]
    owners = out_ref.shape[0]
    capacity = rows // owners
    groups = rows // 128
    slots = member_ref.shape[0] * 128
    per_owner = slots // owners

    block = pl.ds(pl.multiple_of(place[1] * groups, 8), groups)
    small = [
        pltpu.make_async_copy(source, target, small_sem.at[index])
        for index, (source, target) in enumerate(
            [
                (member_hbm, member_ref),
                (request_hbm.at[block, :], request_ref),
                (gain_hbm, gain_ref),
                (position_hbm.at[block, :], position_ref),
                (bias_hbm, bias_ref),
                (freq_hbm, freq_ref),
            ]
        )
    ]
    for copy in small:
        copy.start()
    whole_weight = pltpu.make_async_copy(weight_hbm, weight_ref, weight_sem)
    whole_weight.start()

    def load(group):
        return pltpu.make_async_copy(
            x_hbm.at[pl.ds(group * 128, 128), :], x_ref.at[group % depth], x_sem.at[group % depth]
        )

    for group in range(2):
        load(group).start()
    for copy in small:
        copy.wait()

    for tile in range(width // 128):
        spread_ref[:, tile * 128 : (tile + 1) * 128] = jnp.broadcast_to(
            gain_ref[tile : tile + 1, :], (16, 128)
        )

    members = member_ref[...]
    filler = jnp.zeros((8 - members.shape[0], 128), jnp.int32)
    turned = to_column(jnp.concatenate([members, filler], axis=0).astype(F32))
    member_column = jnp.concatenate(
        [
            jnp.broadcast_to(turned[:, part : part + 1], (128, 128))
            for part in range(slots // 128)
        ],
        axis=0,
    )
    pick_row = iota((32, slots), 0)
    pick_slot = iota((32, slots), 1)
    pick = jnp.where(pick_row == owners, pick_slot % per_owner, 0)
    pick = jnp.where((pick_row < owners) & (pick_slot // per_owner == pick_row), 1, pick)
    pick = pick.astype(F32).astype(BF16)
    earlier = as_mask(iota((128, 128), 0) < iota((128, 128), 1))
    ones = jnp.ones((128, 128), BF16)
    carry = (iota((owners, 128), 0) * capacity).astype(F32)
    ids = jnp.zeros((8, rows), F32)
    for group in range(groups):
        held = as_mask(member_column == request_ref[group : group + 1, :].astype(F32))
        found = nn_dot(pick, held)
        owner_hot = found[:owners]
        hot = owner_hot.astype(BF16)
        ranks = nn_dot(hot, earlier) + carry
        carry = carry + nn_dot(hot, ones)
        target = jnp.sum(owner_hot * ranks, axis=0, keepdims=True).astype(jnp.int32)
        chosen = as_mask(iota((rows, 128), 0) == target)
        perm_ref[group] = chosen
        ids = ids + nt_dot(found[owners : owners + 8].astype(BF16), chosen)

    positions = jnp.where(place[0] == 0, position_ref[...], 0)
    position_columns = 32.0 * to_column((positions >> 5).astype(F32)) + to_column(
        (positions & 31).astype(F32)
    )
    lane = iota((128, 128), 1)

    whole_weight.wait()
    for group in range(2, depth):
        load(group).start()
    piece = 1024
    for group in range(groups):
        load(group).wait()
        product = jnp.zeros((128, 128), F32)
        total = jnp.zeros((128, 128), F32)
        for start in range(0, width, piece):
            raw = x_ref[group % depth, :, start : start + piece]
            squares = raw * raw
            part = squares[:, :128]
            for tile in range(1, piece // 128):
                part = part + squares[:, tile * 128 : (tile + 1) * 128]
            total = total + part.astype(F32)
            gained = raw.reshape(8, 16, piece) * spread_ref[:, start : start + piece][None]
            product = product + nn_dot(
                gained.reshape(128, piece), weight_ref[start : start + piece, :]
            )
        if group + depth < groups:
            load(group + depth).start()
        mean = jnp.sum(total, axis=1, keepdims=True) / width
        scaled = product * lax.rsqrt(mean + EPSILON) + bias_ref[...].astype(F32)
        angles = position_columns[:, group : group + 1] * freq_ref[...]
        quarter = jnp.floor(angles * (2.0 / math.pi) + 0.5)
        rest = angles - quarter * 1.5703125
        rest = rest - quarter * 4.837512969970703125e-4
        rest = rest - quarter * 7.54978995489188216e-8
        square = rest * rest
        sine = rest + rest * square * (
            -1.6666654611e-1 + square * (8.3321608736e-3 + square * -1.9515295891e-4)
        )
        cosine = (
            1.0
            - 0.5 * square
            + square
            * square
            * (
                4.166664568298827e-2
                + square * (-1.388731625493765e-3 + square * 2.443315711809948e-5)
            )
        )
        turn = quarter.astype(jnp.int32) + jnp.where(lane < 64, 1, 0)
        table = jnp.where((turn & 1) == 1, cosine, sine)
        table = jnp.where((turn & 2) == 2, -table, table)
        swapped = pltpu.roll(table, 64, axis=1)
        cosines = jnp.where(lane < 64, table, swapped)
        sines = jnp.where(lane < 64, -swapped, table)
        rotated = scaled * cosines + pltpu.roll(scaled, 64, axis=1) * sines
        rounded_ref[group * 128 : (group + 1) * 128, :] = rotated.astype(BF16)

    everything = jnp.concatenate([perm_ref[group] for group in range(groups)], axis=1)
    ordered = nn_dot(everything, rounded_ref[...]).astype(BF16)
    lanes = iota((16, 128), 1)
    for owner in range(owners):
        out_ref[owner, :capacity, :] = ordered[owner * capacity : (owner + 1) * capacity]
        pair = owner // 2
        both = jnp.broadcast_to(ids[0:1, pair * 128 : (pair + 1) * 128], (16, 128))
        other = pltpu.roll(both, 64, axis=1)
        mine = (lanes < 64) if owner % 2 == 0 else (lanes >= 64)
        out_ref[owner, capacity:, :] = jnp.where(mine, both, other).astype(BF16)


def prefill(place, span_x, norm_gain, weight, bias, span_req, span_pos, members, owners):
    rows, width = span_x.shape
    head_dim = weight.shape[1]
    groups = rows // 128
    half = head_dim // 2
    depth = 4
    freq = (THETA_BASE ** (-(np.arange(head_dim) % half) / half)).astype(np.float32)[None, :]
    small = [
        norm_gain.reshape(-1, 128),
        bias,
        jnp.asarray(freq),
        span_req.reshape(-1, 128),
        span_pos.reshape(-1, 128),
        members.reshape(-1, 128),
    ]
    held = [small[0].shape, small[1].shape, small[2].shape]
    held += [(groups, 128), (groups, 128), small[5].shape]
    return pl.pallas_call(
        prefill_kernel,
        out_shape=jax.ShapeDtypeStruct((owners, rows // owners + 16, head_dim), BF16),
        in_specs=[pl.BlockSpec(memory_space=pltpu.SMEM)] + [pl.BlockSpec(memory_space=pl.ANY)] * 8,
        out_specs=pl.BlockSpec(memory_space=pltpu.VMEM),
        scratch_shapes=[
            pltpu.VMEM((depth, 128, width), BF16),
            pltpu.VMEM((width, head_dim), BF16),
        ]
        + [pltpu.VMEM(shape, array.dtype) for shape, array in zip(held, small)]
        + [
            pltpu.VMEM((16, width), BF16),
            pltpu.VMEM((groups, rows, 128), BF16),
            pltpu.VMEM((rows, head_dim), BF16),
            pltpu.SemaphoreType.DMA((depth,)),
            pltpu.SemaphoreType.DMA,
            pltpu.SemaphoreType.DMA((len(small),)),
        ],
        compiler_params=pltpu.CompilerParams(vmem_limit_bytes=60 * MIB),
        cost_estimate=pl.CostEstimate(
            flops=2 * rows * width * head_dim, bytes_accessed=2 * rows * width, transcendentals=0
        ),
        name="prefill",
    )(place, span_x, weight, *small)


def attention_kernel(
    place, members, cache_len, query_ref, cache_ref, fresh_ref, row_ref, out_ref, q_ref, s_ref, p_ref, sum_ref, acc_ref
):
    steps, slots, heads, dim = query_ref.shape
    per_slot = steps * heads
    rows = slots * per_slot
    cached = cache_ref.shape[1]
    blocks = row_ref.shape[0] // 2
    capacity = row_ref.shape[1] - 16
    spanned = blocks * capacity
    newest = fresh_ref.shape[0]
    scale = 1.0 / math.sqrt(dim)
    for slot in range(slots):
        q_ref[slot * per_slot : (slot + 1) * per_slot, :] = jnp.concatenate(
            [query_ref[step, slot].astype(F32) for step in range(steps)], axis=0
        ).astype(BF16)
    column = iota((per_slot, cached), 1)
    for slot in range(slots):
        span = pl.ds(slot * per_slot, per_slot)
        scores = nt_dot(q_ref[span, :], cache_ref[slot]) * scale
        owner = place[0] * (members.shape[0] // slots // 2) + place[1]
        length = cache_len[members[owner * slots + slot]]
        keep = ((column & 1) == 0) & (column < 2 * length)
        s_ref[span, :cached] = jnp.where(keep, scores, NEGATIVE)
    keys = [row_ref[block, :capacity, :] for block in range(blocks)]
    values = [row_ref[blocks + block, :capacity, :] for block in range(blocks)]
    lane = iota((16, 128), 1)
    row_slot = iota((rows, 128), 0) // per_slot
    for pair in range(spanned // 128):
        scores = nt_dot(q_ref[...], jnp.concatenate(keys[2 * pair : 2 * pair + 2], axis=0)) * scale
        left = row_ref[2 * pair, capacity:, :].astype(F32)
        right = row_ref[2 * pair + 1, capacity:, :].astype(F32)
        ids = jnp.where(lane < 64, left, right)[0:1].astype(jnp.int32)
        s_ref[:, cached + pair * 128 : cached + (pair + 1) * 128] = jnp.where(
            row_slot == ids, scores, NEGATIVE
        )
    row = iota((rows, newest), 0)
    col = iota((rows, newest), 1)
    per_step = 2 * slots
    keep = (
        ((col & 1) == 0)
        & ((col % per_step) // 2 == row // per_slot)
        & (col // per_step <= (row % per_slot) // heads)
    )
    scores = nt_dot(q_ref[...], fresh_ref[...]) * scale
    s_ref[:, cached + spanned :] = jnp.where(keep, scores, NEGATIVE)
    for slot in range(slots):
        span = pl.ds(slot * per_slot, per_slot)
        scores = s_ref[span, :]
        top = jnp.max(scores, axis=1, keepdims=True)
        weights = jnp.exp(scores - top)
        sum_ref[span, :] = jnp.broadcast_to(jnp.sum(weights, axis=1, keepdims=True), (per_slot, dim))
        p_ref[span, :cached] = pltpu.roll(weights[:, :cached], 1, axis=1).astype(BF16)
        p_ref[span, cached : cached + spanned] = weights[:, cached : cached + spanned].astype(BF16)
        p_ref[span, cached + spanned :] = pltpu.roll(
            weights[:, cached + spanned :], 1, axis=1
        ).astype(BF16)
    acc_ref[...] = nn_dot(
        p_ref[:, cached : cached + spanned], jnp.concatenate(values, axis=0)
    ) + nn_dot(p_ref[:, cached + spanned :], fresh_ref[...])
    for slot in range(slots):
        span = pl.ds(slot * per_slot, per_slot)
        acc_ref[span, :] = (
            acc_ref[span, :] + nn_dot(p_ref[span, :cached], cache_ref[slot])
        ) / sum_ref[span, :]
    for head in range(heads):
        out_ref[head] = acc_ref[pl.ds(head, slots * steps, stride=heads), :].astype(BF16)


def attend(place, members, cache_len, queries, cache, fresh, rows):
    steps, slots, heads, dim = queries.shape
    count = slots * steps * heads
    cached = cache.shape[1]
    spanned = (rows.shape[0] // 2) * (rows.shape[1] - 16)
    columns = cached + spanned + fresh.shape[0]
    vmem = pl.BlockSpec(memory_space=pltpu.VMEM)
    return pl.pallas_call(
        attention_kernel,
        out_shape=jax.ShapeDtypeStruct((heads, slots * steps, dim), BF16),
        in_specs=[pl.BlockSpec(memory_space=pltpu.SMEM)] * 3 + [vmem] * 4,
        out_specs=vmem,
        scratch_shapes=[
            pltpu.VMEM((count, dim), BF16),
            pltpu.VMEM((count, columns), F32),
            pltpu.VMEM((count, columns), BF16),
            pltpu.VMEM((count, dim), F32),
            pltpu.VMEM((count, dim), F32),
        ],
        compiler_params=pltpu.CompilerParams(vmem_limit_bytes=32 * MIB),
        name="attend",
    )(place, members, cache_len, queries, cache, fresh, rows)


AXES = ("role", "batch", "tensor")


def gather_round(k):
    pairs = []
    for source in range(128):
        role, batch, tensor = source // 64, source // 8 % 8, source % 8
        x_lo, z, y, x_hi = batch // 4, batch % 4, tensor // 2, tensor % 2
        to_x_lo = x_lo ^ (k >> 2)
        to_z = 2 * (x_hi ^ (k >> 1 & 1)) + ((z & 1) ^ (k & 1))
        pairs.append((source, role * 64 + (to_x_lo * 4 + to_z) * 8 + y * 2 + z // 2))
    return pairs


def project_kernel(place, mine_ref, other_ref, own_ref, partner_ref, *rest):
    outs, staged = rest[:4], rest[4]
    role, batch, tensor = place[0], place[1], place[2]
    x_lo, z_top, z_low = batch >> 2, (batch >> 1) & 1, batch & 1
    y, x_hi = tensor >> 1, tensor & 1
    heads, rows, _ = mine_ref.shape[1:]

    def wide(ref, top):
        blocks = []
        for k in range(8):
            if (k >> 1 & 1) == top:
                blocks.append(
                    jnp.concatenate([ref[k, head] for head in range(heads)], axis=1)
                )
        return jnp.concatenate(blocks, axis=0)

    def work(first, second):
        for step, ref in enumerate((mine_ref, other_ref)):
            product = nn_dot(wide(ref, 0), first[...]) + nn_dot(wide(ref, 1), second[...])
            for index in range(4):
                row_y = 2 * (role ^ step) + (x_lo ^ (index >> 1))
                start = pl.multiple_of((z_low ^ (index & 1)) * rows, rows)
                staged[row_y ^ y, pl.ds(start, rows), :] = product[
                    index * rows : (index + 1) * rows
                ].astype(BF16)

    @pl.when(z_top == x_hi)
    def _():
        work(own_ref, partner_ref)

    @pl.when(z_top != x_hi)
    def _():
        work(partner_ref, own_ref)

    for turn in range(4):
        outs[turn][...] = staged[turn]


def project_out(place, mine, other, own, partner):
    _, heads, rows, _ = mine.shape
    columns = own.shape[1]
    vmem = pl.BlockSpec(memory_space=pltpu.VMEM)
    return pl.pallas_call(
        project_kernel,
        out_shape=[jax.ShapeDtypeStruct((2 * rows, columns), BF16)] * 4,
        in_specs=[pl.BlockSpec(memory_space=pltpu.SMEM)] + [vmem] * 4,
        out_specs=[vmem] * 4,
        scratch_shapes=[pltpu.VMEM((4, 2 * rows, columns), BF16)],
        compiler_params=pltpu.CompilerParams(vmem_limit_bytes=32 * MIB),
        name="project_out",
    )(place, mine, other, own, partner)


def body(
    span_x,
    norm_gain,
    key_value_weight,
    key_value_bias,
    queries,
    decode_key_value,
    kv_cache,
    w_out,
    members,
    span_req,
    span_pos,
    cache_len,
):
    n_role = lax.axis_size("role")
    n_batch = lax.axis_size("batch")
    owners = n_role * n_batch
    my_role = lax.axis_index("role")
    my_batch = lax.axis_index("batch")
    width = span_x.shape[1]
    head_dim = key_value_weight.shape[3]
    steps, slots, heads, _ = queries.shape
    place = jnp.stack([my_role, my_batch, lax.axis_index("tensor")]).astype(jnp.int32)
    partner = lax.ppermute(w_out, "tensor", [(t, t ^ 1) for t in range(8)])
    outgoing = prefill(
        place,
        span_x,
        norm_gain,
        key_value_weight.reshape(width, head_dim),
        key_value_bias.reshape(1, head_dim),
        span_req,
        span_pos,
        members,
        owners,
    )
    arrived = lax.all_to_all(outgoing, ("role", "batch"), 0, 0)
    attention = attend(
        place,
        members,
        cache_len,
        queries,
        kv_cache.reshape(slots, -1, head_dim),
        decode_key_value.reshape(-1, head_dim),
        arrived,
    )

    gathered = jnp.stack([lax.ppermute(attention, AXES, gather_round(k)) for k in range(8)])
    other = lax.ppermute(gathered, "role", [(0, 1), (1, 0)])
    parts = project_out(place, gathered, other, w_out, partner)
    total = parts[0].astype(F32)
    for turn in range(1, 4):
        total = total + lax.ppermute(
            parts[turn], "tensor", [(t, t ^ (2 * turn)) for t in range(8)]
        ).astype(F32)
    return total.astype(BF16).reshape(-1, steps, w_out.shape[1])


def solution(mesh):
    placed = (
        P("batch", None),
        P(),
        P(None, "tensor", "role", None),
        P("tensor", "role", None),
        P(None, ("role", "batch"), "tensor", None),
        P(None, ("role", "batch"), "tensor", None, None),
        P(("role", "batch"), None, "tensor", None, None),
        P("tensor", ("role", "batch")),
        P(),
        P(),
        P(),
        P(),
    )
    return jax.shard_map(
        body,
        mesh=mesh,
        in_specs=placed,
        out_specs=P("tensor", None, ("role", "batch")),
        check_vma=False,
    )
```

time: 94.1 us -> 116 us (1.23)
  the two profiles are of different devices: /device:TPU:0 before, /device:TPU:6 now
where the time goes in v2:
time: 116 us; the launch traced here: 115 us
  waiting for transfers between devices  62.2 us (54%)
  Pallas kernels  18.7 us (16%)
  starting transfers between devices  18 us (16%)
  blocking collectives  14.6 us (13%)
    ppermute x8, waiting for transfers between devices, body(): lax.ppermute(attention, AXES, gather_round(k))  51.1 us
    all_to_all x1, blocking collectives, body(): arrived = lax.all_to_all(outgoing, ('role', 'batch'), 0, 0)  14.6 us
    pallas_call x1, Pallas kernels, prefill(): pl.pallas_call(prefill_kernel, out_shape=jax.ShapeDtypeStruct((owners, ro...  14.2 us
    ppermute x8, starting transfers between devices, body(): lax.ppermute(attention, AXES, gather_round(k))  13.1 us
    ppermute x3, waiting for transfers between devices, body(): lax.ppermute(parts[turn], 'tensor', [(t, t ^ 2 * turn) for t in range(8)])  8.43 us
    ppermute x3, starting transfers between devices, body(): lax.ppermute(parts[turn], 'tensor', [(t, t ^ 2 * turn) for t in range(8)])  4.78 us
    pallas_call x1, Pallas kernels, attend(): pl.pallas_call(attention_kernel, out_shape=jax.ShapeDtypeStruct((heads, s...  2.72 us
    ppermute x1, waiting for transfers between devices, body(): other = lax.ppermute(gathered, 'role', [(0, 1), (1, 0)])  2.64 us
  transfers between devices with their start and end apart: 13, of which 9 were waited for; matrix products, arithmetic and copies ran while one was open for 0% of the time, Pallas kernels for 0%

profile of v2, /device:TPU:6, one launch (start us, length us, event | category | flops | bytes accessed | tf_op | source)
XLA Modules:
  0.0 115.3 jit_solution(3573338781324236944)
XLA Ops:
  0.0 0.6 pad_add_fusion.place
  0.7 14.2 %prefill.1 = bf16[16,80,128]{2,1,0:T(8,128)(2,1)} custom-call(s32[3]{0:T(128)} %pad_add_fusion.place, bf16[1024,8192]{1,0:T(8,128)(2,1)} %x_hbm.1, bf16[8192,128]{1,0:T(8,128)(2,1)} %bitcast.30, bf16[64,128]{1,0:T(8,128)(2,1)} %bitcast.33, bf16[1,128]{1,0:T(2,128)(2,1)} %bitcast.34, f32[1,128]{1,0:T(1,128)} %constant.15.clone.freq_hbm, s32[64,128]{1,0:T(8,128)} %bitcast.31, ...), custom_call_target="tpu_custom_call" | custom-call | flops 2147483648 | bytes 16777216 | tf_op jit(solution)/shard_map/prefill/pallas_call | solution.py:226
  14.9 14.6 %all_to_all.5.row_ref = bf16[16,80,128]{2,1,0:T(8,128)(2,1)S(1)} all-to-all(bf16[16,80,128]{2,1,0:T(8,128)(2,1)} %prefill.1), channel_id=1, replica_groups=mesh['role'=2,'batch'=8,'tensor'=8] {'role','batch'}, dimensions={0} | all-to-all | bytes 655360 | tf_op jit(solution)/shard_map/all_to_all | solution.py:447
  29.5 2.7 %attend.1 = bf16[8,64,128]{2,1,0:T(8,128)(2,1)S(1)} custom-call(s32[3]{0:T(128)S(1)} %copy-done.4, s32[256]{0:T(256)S(1)} %copy-done.5, s32[256]{0:T(256)S(1)} %copy-done.6, bf16[4,16,8,128]{3,2,1,0:T(8,128)(2,1)S(1)} %copy-done.2, bf16[16,512,128]{2,1,0:T(8,128)(2,1)S(1)} %bitcast.27, bf16[128,128]{1,0:T(8,128)(2,1)S(1)} %bitcast.28, ...), custom_call_target="tpu_custom_call" | custom-call | tf_op jit(solution)/shard_map/attend/pallas_call | solution.py:328
  32.2 3.5 %collective-permute-start = (bf16[8,64,128]{2,1,0:T(8,128)(2,1)S(1)}, bf16[8,64,128]{2,1,0:T(8,128)(2,1)S(1)}, u32[]{:S(2)}, u32[]{:S(2)}) collective-permute-start(bf16[8,64,128]{2,1,0:T(8,128)(2,1)S(1)} %attend.1), channel_id=1, source_target_pairs={{0,0},{1,16},{2,2},{3,18},{4,4},{5,20},{6,6},{7,22},{8,8},{9,24},{... | collective-permute-start | bytes 393224 | tf_op jit(solution)/shard_map/ppermute | solution.py:458
  35.8 0.1 collective-permute-start.9
  35.9 3.4 %collective-permute-start.7 = (bf16[8,64,128]{2,1,0:T(8,128)(2,1)S(1)}, bf16[8,64,128]{2,1,0:T(8,128)(2,1)S(1)}, u32[]{:S(2)}, u32[]{:S(2)}) collective-permute-start(bf16[8,64,128]{2,1,0:T(8,128)(2,1)S(1)} %attend.1), channel_id=1, source_target_pairs={{0,56},{1,40},{2,58},{3,42},{4,60},{5,44},{6,62},{7,46},{8,48},{9,... | collective-permute-start | bytes 393224 | tf_op jit(solution)/shard_map/ppermute | solution.py:458
  39.2 1.3 %collective-permute-start.6 = (bf16[8,64,128]{2,1,0:T(8,128)(2,1)S(1)}, bf16[8,64,128]{2,1,0:T(8,128)(2,1)S(1)}, u32[]{:S(2)}, u32[]{:S(2)}) collective-permute-start(bf16[8,64,128]{2,1,0:T(8,128)(2,1)S(1)} %attend.1), channel_id=1, source_target_pairs={{0,48},{1,32},{2,50},{3,34},{4,52},{5,36},{6,54},{7,38},{8,56},{9,... | collective-permute-start | bytes 393224 | tf_op jit(solution)/shard_map/ppermute | solution.py:458
  40.5 2.9 %collective-permute-start.5 = (bf16[8,64,128]{2,1,0:T(8,128)(2,1)S(1)}, bf16[8,64,128]{2,1,0:T(8,128)(2,1)S(1)}, u32[]{:S(2)}, u32[]{:S(2)}) collective-permute-start(bf16[8,64,128]{2,1,0:T(8,128)(2,1)S(1)} %attend.1), channel_id=1, source_target_pairs={{0,40},{1,56},{2,42},{3,58},{4,44},{5,60},{6,46},{7,62},{8,32},{9,... | collective-permute-start | bytes 393224 | tf_op jit(solution)/shard_map/ppermute | solution.py:458
  43.4 1.2 %collective-permute-done = bf16[8,64,128]{2,1,0:T(8,128)(2,1)S(1)} collective-permute-done((bf16[8,64,128]{2,1,0:T(8,128)(2,1)S(1)}, bf16[8,64,128]{2,1,0:T(8,128)(2,1)S(1)}, u32[]{:S(2)}, u32[]{:S(2)}) %collective-permute-start) | collective-permute-done | bytes 131104 | tf_op jit(solution)/shard_map/ppermute | solution.py:458
  44.6 2.0 %collective-permute-start.1 = (bf16[8,64,128]{2,1,0:T(8,128)(2,1)S(1)}, bf16[8,64,128]{2,1,0:T(8,128)(2,1)S(1)}, u32[]{:S(2)}, u32[]{:S(2)}) collective-permute-start(bf16[8,64,128]{2,1,0:T(8,128)(2,1)S(1)} %attend.1), channel_id=1, source_target_pairs={{0,8},{1,24},{2,10},{3,26},{4,12},{5,28},{6,14},{7,30},{8,0},{9,16... | collective-permute-start | bytes 393224 | tf_op jit(solution)/shard_map/ppermute | solution.py:458
  46.6 23.1 %collective-permute-done.1 = bf16[8,64,128]{2,1,0:T(8,128)(2,1)S(1)} collective-permute-done((bf16[8,64,128]{2,1,0:T(8,128)(2,1)S(1)}, bf16[8,64,128]{2,1,0:T(8,128)(2,1)S(1)}, u32[]{:S(2)}, u32[]{:S(2)}) %collective-permute-start.1) | collective-permute-done | bytes 131104 | tf_op jit(solution)/shard_map/ppermute | solution.py:458
  69.7 12.0 %collective-permute-done.2 = bf16[8,64,128]{2,1,0:T(8,128)(2,1)S(1)} collective-permute-done((bf16[8,64,128]{2,1,0:T(8,128)(2,1)S(1)}, bf16[8,64,128]{2,1,0:T(8,128)(2,1)S(1)}, u32[]{:S(2)}, u32[]{:S(2)}) %collective-permute-start.2) | collective-permute-done | bytes 131104 | tf_op jit(solution)/shard_map/ppermute | solution.py:458
  81.7 6.3 %collective-permute-done.3 = bf16[8,64,128]{2,1,0:T(8,128)(2,1)S(1)} collective-permute-done((bf16[8,64,128]{2,1,0:T(8,128)(2,1)S(1)}, bf16[8,64,128]{2,1,0:T(8,128)(2,1)S(1)}, u32[]{:S(2)}, u32[]{:S(2)}) %collective-permute-start.3) | collective-permute-done | bytes 131104 | tf_op jit(solution)/shard_map/ppermute | solution.py:458
  88.1 8.6 %collective-permute-done.4 = bf16[8,64,128]{2,1,0:T(8,128)(2,1)S(1)} collective-permute-done((bf16[8,64,128]{2,1,0:T(8,128)(2,1)S(1)}, bf16[8,64,128]{2,1,0:T(8,128)(2,1)S(1)}, u32[]{:S(2)}, u32[]{:S(2)}) %collective-permute-start.4) | collective-permute-done | bytes 131104 | tf_op jit(solution)/shard_map/ppermute | solution.py:458
  96.8 2.6 %collective-permute-done.8.other_ref = bf16[8,8,64,128]{3,2,1,0:T(8,128)(2,1)S(1)} collective-permute-done((bf16[8,8,64,128]{3,2,1,0:T(8,128)(2,1)S(1)}, bf16[8,8,64,128]{3,2,1,0:T(8,128)(2,1)S(1)}, u32[]{:S(2)}, u32[]{:S(2)}) %collective-permute-start.8) | collective-permute-done | bytes 1048608 | tf_op jit(solution)/shard_map/ppermute | solution.py:459
  99.5 1.8 %project_out.1 = (bf16[128,512]{1,0:T(8,128)(2,1)S(1)}, bf16[128,512]{1,0:T(8,128)(2,1)S(1)}, bf16[128,512]{1,0:T(8,128)(2,1)S(1)}, bf16[128,512]{1,0:T(8,128)(2,1)S(1)}) custom-call(s32[3]{0:T(128)S(1)} %copy-done.4, bf16[8,8,64,128]{3,2,1,0:T(8,128)(2,1)S(1)} %bitcast_dynamic-update-slice_fusion.mine_ref, ...), custom_call_target="tpu_custom_call" | custom-call | tf_op jit(solution)/shard_map/project_out/pallas_call | solution.py:401
  101.3 1.6 %collective-permute-start.10 = (bf16[128,512]{1,0:T(8,128)(2,1)S(1)}, bf16[128,512]{1,0:T(8,128)(2,1)S(1)}, u32[]{:S(2)}, u32[]{:S(2)}) collective-permute-start(bf16[128,512]{1,0:T(8,128)(2,1)S(1)} %get-tuple-element.10), channel_id=1, source_target_pairs={{0,2},{1,3},{2,0},{3,1},{4,6},{5,7},{6,4},{7,5},{8,10},{9,11},{10,... | collective-permute-start | bytes 393224 | tf_op jit(solution)/shard_map/ppermute | solution.py:463
  103.0 2.9 %collective-permute-start.11 = (bf16[128,512]{1,0:T(8,128)(2,1)S(1)}, bf16[128,512]{1,0:T(8,128)(2,1)S(1)}, u32[]{:S(2)}, u32[]{:S(2)}) collective-permute-start(bf16[128,512]{1,0:T(8,128)(2,1)S(1)} %get-tuple-element.11), channel_id=1, source_target_pairs={{0,4},{1,5},{2,6},{3,7},{4,0},{5,1},{6,2},{7,3},{8,12},{9,13},{10,... | collective-permute-start | bytes 393224 | tf_op jit(solution)/shard_map/ppermute | solution.py:463
  105.9 0.2 collective-permute-start.12
  106.1 1.3 %collective-permute-done.10 = bf16[128,512]{1,0:T(8,128)(2,1)S(1)} collective-permute-done((bf16[128,512]{1,0:T(8,128)(2,1)S(1)}, bf16[128,512]{1,0:T(8,128)(2,1)S(1)}, u32[]{:S(2)}, u32[]{:S(2)}) %collective-permute-start.10) | collective-permute-done | bytes 131104 | tf_op jit(solution)/shard_map/ppermute | solution.py:463
  107.4 4.9 %collective-permute-done.11 = bf16[128,512]{1,0:T(8,128)(2,1)S(1)} collective-permute-done((bf16[128,512]{1,0:T(8,128)(2,1)S(1)}, bf16[128,512]{1,0:T(8,128)(2,1)S(1)}, u32[]{:S(2)}, u32[]{:S(2)}) %collective-permute-start.11) | collective-permute-done | bytes 131104 | tf_op jit(solution)/shard_map/ppermute | solution.py:463
  112.3 2.2 %collective-permute-done.12 = bf16[128,512]{1,0:T(8,128)(2,1)S(1)} collective-permute-done((bf16[128,512]{1,0:T(8,128)(2,1)S(1)}, bf16[128,512]{1,0:T(8,128)(2,1)S(1)}, u32[]{:S(2)}, u32[]{:S(2)}) %collective-permute-start.12) | collective-permute-done | bytes 131104 | tf_op jit(solution)/shard_map/ppermute | solution.py:463
  114.6 0.7 reshape.35
  (31 shorter events, 0.3 us)
Async XLA Ops:
  0.6 28.8 %copy-start = (bf16[16,256,1,2,128]{4,3,2,1,0:T(2,128)(2,1)S(1)}, bf16[16,256,1,2,128]{4,3,2,1,0:T(2,128)(2,1)}, u32[]{:S(2)}) copy-start(bf16[16,256,1,2,128]{4,3,2,1,0:T(2,128)(2,1)} %param.19) | copy-start | bytes 6291460
  0.6 28.8 %copy-start.2 = (bf16[4,16,8,128]{3,2,1,0:T(8,128)(2,1)S(1)}, bf16[4,16,8,128]{3,2,1,0:T(8,128)(2,1)}, u32[]{:S(2)}) copy-start(bf16[4,16,8,128]{3,2,1,0:T(8,128)(2,1)} %query_ref.1) | copy-start | bytes 393220
  0.6 28.8 %copy-start.3 = (bf16[4,16,1,2,128]{4,3,2,1,0:T(2,128)(2,1)S(1)}, bf16[4,16,1,2,128]{4,3,2,1,0:T(2,128)(2,1)}, u32[]{:S(2)}) copy-start(bf16[4,16,1,2,128]{4,3,2,1,0:T(2,128)(2,1)} %param.18) | copy-start | bytes 98308
  0.6 28.8 %copy-start.4 = (s32[3]{0:T(128)S(1)}, s32[3]{0:T(128)}, u32[]{:S(2)}) copy-start(s32[3]{0:T(128)} %pad_add_fusion.place) | copy-start | bytes 40
  0.7 28.8 %copy-start.5 = (s32[256]{0:T(256)S(1)}, s32[256]{0:T(256)}, u32[]{:S(2)}) copy-start(s32[256]{0:T(256)} %members.1) | copy-start | bytes 3076
  0.7 28.8 %copy-start.6 = (s32[256]{0:T(256)S(1)}, s32[256]{0:T(256)}, u32[]{:S(2)}) copy-start(s32[256]{0:T(256)} %cache_len.1) | copy-start | bytes 3076
  14.8 20.9 %copy-start.1 = (bf16[1024,512]{1,0:T(8,128)(2,1)S(1)}, bf16[1024,512]{1,0:T(8,128)(2,1)}, u32[]{:S(2)}) copy-start(bf16[1024,512]{1,0:T(8,128)(2,1)} %own_ref.1) | copy-start | bytes 3145732
  32.2 12.3 %collective-permute-start = (bf16[8,64,128]{2,1,0:T(8,128)(2,1)S(1)}, bf16[8,64,128]{2,1,0:T(8,128)(2,1)S(1)}, u32[]{:S(2)}, u32[]{:S(2)}) collective-permute-start(bf16[8,64,128]{2,1,0:T(8,128)(2,1)S(1)} %attend.1), channel_id=1, source_target_pairs={{0,0},{1,16},{2,2},{3,18},{4,4},{5,20},{6,6},{7,22},{8,8},{9,24},{... | collective-permute-start | bytes 393224 | tf_op jit(solution)/shard_map/ppermute | solution.py:458
  35.8 61.1 %collective-permute-start.9 = (bf16[1024,512]{1,0:T(8,128)(2,1)S(1)}, bf16[1024,512]{1,0:T(8,128)(2,1)S(1)}, u32[]{:S(2)}, u32[]{:S(2)}) collective-permute-start(bf16[1024,512]{1,0:T(8,128)(2,1)S(1)} %copy-done.1), channel_id=1, source_target_pairs={{0,1},{1,0},{2,3},{3,2},{4,5},{5,4},{6,7},{7,6},{8,9},{9,8},{10,11... | collective-permute-start | bytes 3145736 | tf_op jit(solution)/shard_map/ppermute | solution.py:435
  35.9 60.8 %collective-permute-start.7 = (bf16[8,64,128]{2,1,0:T(8,128)(2,1)S(1)}, bf16[8,64,128]{2,1,0:T(8,128)(2,1)S(1)}, u32[]{:S(2)}, u32[]{:S(2)}) collective-permute-start(bf16[8,64,128]{2,1,0:T(8,128)(2,1)S(1)} %attend.1), channel_id=1, source_target_pairs={{0,56},{1,40},{2,58},{3,42},{4,60},{5,44},{6,62},{7,46},{8,48},{9,... | collective-permute-start | bytes 393224 | tf_op jit(solution)/shard_map/ppermute | solution.py:458
  39.2 57.4 %collective-permute-start.6 = (bf16[8,64,128]{2,1,0:T(8,128)(2,1)S(1)}, bf16[8,64,128]{2,1,0:T(8,128)(2,1)S(1)}, u32[]{:S(2)}, u32[]{:S(2)}) collective-permute-start(bf16[8,64,128]{2,1,0:T(8,128)(2,1)S(1)} %attend.1), channel_id=1, source_target_pairs={{0,48},{1,32},{2,50},{3,34},{4,52},{5,36},{6,54},{7,38},{8,56},{9,... | collective-permute-start | bytes 393224 | tf_op jit(solution)/shard_map/ppermute | solution.py:458
  40.5 56.1 %collective-permute-start.5 = (bf16[8,64,128]{2,1,0:T(8,128)(2,1)S(1)}, bf16[8,64,128]{2,1,0:T(8,128)(2,1)S(1)}, u32[]{:S(2)}, u32[]{:S(2)}) collective-permute-start(bf16[8,64,128]{2,1,0:T(8,128)(2,1)S(1)} %attend.1), channel_id=1, source_target_pairs={{0,40},{1,56},{2,42},{3,58},{4,44},{5,60},{6,46},{7,62},{8,32},{9,... | collective-permute-start | bytes 393224 | tf_op jit(solution)/shard_map/ppermute | solution.py:458
  44.6 25.1 %collective-permute-start.1 = (bf16[8,64,128]{2,1,0:T(8,128)(2,1)S(1)}, bf16[8,64,128]{2,1,0:T(8,128)(2,1)S(1)}, u32[]{:S(2)}, u32[]{:S(2)}) collective-permute-start(bf16[8,64,128]{2,1,0:T(8,128)(2,1)S(1)} %attend.1), channel_id=1, source_target_pairs={{0,8},{1,24},{2,10},{3,26},{4,12},{5,28},{6,14},{7,30},{8,0},{9,16... | collective-permute-start | bytes 393224 | tf_op jit(solution)/shard_map/ppermute | solution.py:458
  69.7 12.0 %collective-permute-start.2 = (bf16[8,64,128]{2,1,0:T(8,128)(2,1)S(1)}, bf16[8,64,128]{2,1,0:T(8,128)(2,1)S(1)}, u32[]{:S(2)}, u32[]{:S(2)}) collective-permute-start(bf16[8,64,128]{2,1,0:T(8,128)(2,1)S(1)} %attend.1), channel_id=1, source_target_pairs={{0,16},{1,0},{2,18},{3,2},{4,20},{5,4},{6,22},{7,6},{8,24},{9,8},{... | collective-permute-start | bytes 393224 | tf_op jit(solution)/shard_map/ppermute | solution.py:458
  81.7 6.3 %collective-permute-start.3 = (bf16[8,64,128]{2,1,0:T(8,128)(2,1)S(1)}, bf16[8,64,128]{2,1,0:T(8,128)(2,1)S(1)}, u32[]{:S(2)}, u32[]{:S(2)}) collective-permute-start(bf16[8,64,128]{2,1,0:T(8,128)(2,1)S(1)} %attend.1), channel_id=1, source_target_pairs={{0,24},{1,8},{2,26},{3,10},{4,28},{5,12},{6,30},{7,14},{8,16},{9,0... | collective-permute-start | bytes 393224 | tf_op jit(solution)/shard_map/ppermute | solution.py:458
  88.0 8.6 %collective-permute-start.4 = (bf16[8,64,128]{2,1,0:T(8,128)(2,1)S(1)}, bf16[8,64,128]{2,1,0:T(8,128)(2,1)S(1)}, u32[]{:S(2)}, u32[]{:S(2)}) collective-permute-start(bf16[8,64,128]{2,1,0:T(8,128)(2,1)S(1)} %attend.1), channel_id=1, source_target_pairs={{0,32},{1,48},{2,34},{3,50},{4,36},{5,52},{6,38},{7,54},{8,40},{9,... | collective-permute-start | bytes 393224 | tf_op jit(solution)/shard_map/ppermute | solution.py:458
  96.7 2.7 %collective-permute-start.8 = (bf16[8,8,64,128]{3,2,1,0:T(8,128)(2,1)S(1)}, bf16[8,8,64,128]{3,2,1,0:T(8,128)(2,1)S(1)}, u32[]{:S(2)}, u32[]{:S(2)}) collective-permute-start(bf16[8,8,64,128]{3,2,1,0:T(8,128)(2,1)S(1)} %bitcast_dynamic-update-slice_fusion.mine_ref), channel_id=1, source_target_pairs={{0,64},{64,0},{1,65},{65,1},{2,66},{66,2},{3,67},{67,3},{4,68},{68... | collective-permute-start | bytes 3145736 | tf_op jit(solution)/shard_map/ppermute | solution.py:459
  101.3 6.1 %collective-permute-start.10 = (bf16[128,512]{1,0:T(8,128)(2,1)S(1)}, bf16[128,512]{1,0:T(8,128)(2,1)S(1)}, u32[]{:S(2)}, u32[]{:S(2)}) collective-permute-start(bf16[128,512]{1,0:T(8,128)(2,1)S(1)} %get-tuple-element.10), channel_id=1, source_target_pairs={{0,2},{1,3},{2,0},{3,1},{4,6},{5,7},{6,4},{7,5},{8,10},{9,11},{10,... | collective-permute-start | bytes 393224 | tf_op jit(solution)/shard_map/ppermute | solution.py:463
  103.0 9.3 %collective-permute-start.11 = (bf16[128,512]{1,0:T(8,128)(2,1)S(1)}, bf16[128,512]{1,0:T(8,128)(2,1)S(1)}, u32[]{:S(2)}, u32[]{:S(2)}) collective-permute-start(bf16[128,512]{1,0:T(8,128)(2,1)S(1)} %get-tuple-element.11), channel_id=1, source_target_pairs={{0,4},{1,5},{2,6},{3,7},{4,0},{5,1},{6,2},{7,3},{8,12},{9,13},{10,... | collective-permute-start | bytes 393224 | tf_op jit(solution)/shard_map/ppermute | solution.py:463
  105.9 8.7 %collective-permute-start.12 = (bf16[128,512]{1,0:T(8,128)(2,1)S(1)}, bf16[128,512]{1,0:T(8,128)(2,1)S(1)}, u32[]{:S(2)}, u32[]{:S(2)}) collective-permute-start(bf16[128,512]{1,0:T(8,128)(2,1)S(1)} %get-tuple-element.12), channel_id=1, source_target_pairs={{0,6},{1,7},{2,4},{3,5},{4,2},{5,3},{6,0},{7,1},{8,14},{9,15},{10,... | collective-permute-start | bytes 393224 | tf_op jit(solution)/shard_map/ppermute | solution.py:463

commit v3 on v2

--- a/solution.py
+++ b/solution.py
@@ -345,68 +345,69 @@
 AXES = ("role", "batch", "tensor")
 
 
-def gather_round(k):
+def places(device):
+    batch, tensor = device // 8 % 8, device % 8
+    return device // 64, batch // 4, batch % 4, tensor // 2, tensor % 2
+
+
+def moves(target):
     pairs = []
     for source in range(128):
-        role, batch, tensor = source // 64, source // 8 % 8, source % 8
-        x_lo, z, y, x_hi = batch // 4, batch % 4, tensor // 2, tensor % 2
-        to_x_lo = x_lo ^ (k >> 2)
-        to_z = 2 * (x_hi ^ (k >> 1 & 1)) + ((z & 1) ^ (k & 1))
-        pairs.append((source, role * 64 + (to_x_lo * 4 + to_z) * 8 + y * 2 + z // 2))
+        role, x_lo, z, y, x_hi = target(*places(source))
+        pairs.append((source, role * 64 + (x_lo * 4 + z) * 8 + y * 2 + x_hi))
     return pairs
 
 
-def project_kernel(place, mine_ref, other_ref, own_ref, partner_ref, *rest):
-    outs, staged = rest[:4], rest[4]
+def sum_round(k):
+    return moves(
+        lambda role, x_lo, z, y, x_hi: (
+            role,
+            (y & 1) ^ (k & 1),
+            z,
+            2 * ((y >> 1) ^ (k >> 2)) + x_lo,
+            x_hi ^ (k >> 1 & 1),
+        )
+    )
+
+
+def project_kernel(place, mine_ref, other_ref, own_ref, x_ref, *rest):
+    outs, staged = rest[:-1], rest[-1]
     role, batch, tensor = place[0], place[1], place[2]
     x_lo, z_top, z_low = batch >> 2, (batch >> 1) & 1, batch & 1
     y, x_hi = tensor >> 1, tensor & 1
-    heads, rows, _ = mine_ref.shape[1:]
-
-    def wide(ref, top):
-        blocks = []
-        for k in range(8):
-            if (k >> 1 & 1) == top:
-                blocks.append(
-                    jnp.concatenate([ref[k, head] for head in range(heads)], axis=1)
-                )
-        return jnp.concatenate(blocks, axis=0)
-
-    def work(first, second):
-        for step, ref in enumerate((mine_ref, other_ref)):
-            product = nn_dot(wide(ref, 0), first[...]) + nn_dot(wide(ref, 1), second[...])
-            for index in range(4):
-                row_y = 2 * (role ^ step) + (x_lo ^ (index >> 1))
-                start = pl.multiple_of((z_low ^ (index & 1)) * rows, rows)
-                staged[row_y ^ y, pl.ds(start, rows), :] = product[
-                    index * rows : (index + 1) * rows
-                ].astype(BF16)
-
-    @pl.when(z_top == x_hi)
-    def _():
-        work(own_ref, partner_ref)
-
-    @pl.when(z_top != x_hi)
-    def _():
-        work(partner_ref, own_ref)
-
-    for turn in range(4):
-        outs[turn][...] = staged[turn]
-
-
-def project_out(place, mine, other, own, partner):
+    blocks, heads, rows, _ = mine_ref.shape
+    for step, ref in enumerate((mine_ref, other_ref)):
+        left = jnp.concatenate(
+            [
+                jnp.concatenate([ref[block, head] for head in range(heads)], axis=1)
+                for block in range(blocks)
+            ],
+            axis=0,
+        )
+        for turn, weight in enumerate((own_ref, x_ref)):
+            product = nn_dot(left, weight[...]).astype(BF16)
+            for block in range(blocks):
+                slot = 4 * (role ^ step ^ (y >> 1))
+                slot += 2 * (z_top ^ (block >> 1) ^ x_hi) + (x_lo ^ turn ^ (y & 1))
+                start = pl.multiple_of((z_low ^ (block & 1)) * rows, rows)
+                staged[slot, pl.ds(start, rows), :] = product[block * rows : (block + 1) * rows]
+    for turn, out in enumerate(outs):
+        out[...] = staged[turn]
+
+
+def project_out(place, mine, other, *weights):
     _, heads, rows, _ = mine.shape
-    columns = own.shape[1]
+    columns = weights[0].shape[1]
     vmem = pl.BlockSpec(memory_space=pltpu.VMEM)
     return pl.pallas_call(
         project_kernel,
-        out_shape=[jax.ShapeDtypeStruct((2 * rows, columns), BF16)] * 4,
+        out_shape=[jax.ShapeDtypeStruct((2 * rows, columns), BF16)] * 8,
         in_specs=[pl.BlockSpec(memory_space=pltpu.SMEM)] + [vmem] * 4,
-        out_specs=[vmem] * 4,
-        scratch_shapes=[pltpu.VMEM((4, 2 * rows, columns), BF16)],
+        out_specs=[vmem] * 8,
+        scratch_shapes=[pltpu.VMEM((8, 2 * rows, columns), BF16)],
         compiler_params=pltpu.CompilerParams(vmem_limit_bytes=32 * MIB),
         name="project_out",
-    )(place, mine, other, own, partner)
+    )(place, mine, other, *weights)
 
 
 def body(
@@ -432,7 +433,7 @@
     head_dim = key_value_weight.shape[3]
     steps, slots, heads, _ = queries.shape
     place = jnp.stack([my_role, my_batch, lax.axis_index("tensor")]).astype(jnp.int32)
-    partner = lax.ppermute(w_out, "tensor", [(t, t ^ 1) for t in range(8)])
+    beside = lax.ppermute(w_out, "batch", [(b, b ^ 4) for b in range(8)])
     outgoing = prefill(
         place,
         span_x,
@@ -445,6 +446,7 @@
         owners,
     )
     arrived = lax.all_to_all(outgoing, ("role", "batch"), 0, 0)
+    arrived, beside = lax.optimization_barrier((arrived, beside))
     attention = attend(
         place,
         members,
@@ -455,14 +457,13 @@
         arrived,
     )
 
-    gathered = jnp.stack([lax.ppermute(attention, AXES, gather_round(k)) for k in range(8)])
+    gathered = jnp.stack(
+        [attention]
+        + [lax.ppermute(attention, "batch", [(b, b ^ k) for b in range(8)]) for k in range(1, 4)]
+    )
     other = lax.ppermute(gathered, "role", [(0, 1), (1, 0)])
-    parts = project_out(place, gathered, other, w_out, partner)
-    total = parts[0].astype(F32)
-    for turn in range(1, 4):
-        total = total + lax.ppermute(
-            parts[turn], "tensor", [(t, t ^ (2 * turn)) for t in range(8)]
-        ).astype(F32)
+    parts = project_out(place, gathered, other, w_out, beside)
+    total = sum(lax.ppermute(parts[k], AXES, sum_round(k)).astype(F32) for k in range(8))
     return total.astype(BF16).reshape(-1, steps, w_out.shape[1])
 
 

time: 116 us -> 76.5 us (0.66)
  the two profiles are of different devices: /device:TPU:6 before, /device:TPU:0 now
where the time goes in v3:
time: 76.5 us; the launch traced here: 76.3 us
  starting transfers between devices  25.1 us (33%)
  Pallas kernels  18.7 us (24%)
  waiting for transfers between devices  15.5 us (20%)
  blocking collectives  15.3 us (20%)
  other arithmetic  0.85 us (1%)
    ppermute x8, starting transfers between devices, body(): lax.ppermute(parts[k], AXES, sum_round(k)).astype(F32)  19.3 us
    all_to_all x1, blocking collectives, body(): arrived = lax.all_to_all(outgoing, ('role', 'batch'), 0, 0)  15.3 us
    pallas_call x1, Pallas kernels, prefill(): pl.pallas_call(prefill_kernel, out_shape=jax.ShapeDtypeStruct((owners, ro...  14.2 us
    ppermute x8, waiting for transfers between devices, body(): lax.ppermute(parts[k], AXES, sum_round(k)).astype(F32)  7.65 us
    ppermute x3, waiting for transfers between devices, body(): lax.ppermute(attention, 'batch', [(b, b ^ k) for b in range(8)])  6 us
    ppermute x3, starting transfers between devices, body(): lax.ppermute(attention, 'batch', [(b, b ^ k) for b in range(8)])  4.17 us
    pallas_call x1, Pallas kernels, attend(): pl.pallas_call(attention_kernel, out_shape=jax.ShapeDtypeStruct((heads, s...  2.63 us
    ppermute x1, waiting for transfers between devices, body(): other = lax.ppermute(gathered, 'role', [(0, 1), (1, 0)])  1.9 us
  transfers between devices with their start and end apart: 13, of which 5 were waited for; matrix products, arithmetic and copies ran while one was open for 1% of the time, Pallas kernels for 19%

profile of v3, /device:TPU:0, one launch (start us, length us, event | category | flops | bytes accessed | tf_op | source)
XLA Modules:
  0.0 76.3 jit_solution(9299994392901391478)
XLA Ops:
  0.0 1.6 %collective-permute-start = (bf16[1024,512]{1,0:T(8,128)(2,1)}, bf16[1024,512]{1,0:T(8,128)(2,1)S(1)}, u32[]{:S(2)}, u32[]{:S(2)}) collective-permute-start(bf16[1024,512]{1,0:T(8,128)(2,1)} %own_ref.1), channel_id=1, source_target_pairs={{0,32},{8,40},{16,48},{24,56},{32,0},{40,8},{48,16},{56,24},{1,33}... | collective-permute-start | bytes 3145736 | tf_op jit(solution)/shard_map/ppermute | solution.py:436
  1.6 0.6 pad_add_fusion.place
  2.3 14.2 %prefill.1 = bf16[16,80,128]{2,1,0:T(8,128)(2,1)} custom-call(s32[3]{0:T(128)} %pad_add_fusion.place, bf16[1024,8192]{1,0:T(8,128)(2,1)} %x_hbm.1, bf16[8192,128]{1,0:T(8,128)(2,1)} %bitcast.19, bf16[64,128]{1,0:T(8,128)(2,1)} %bitcast.25, bf16[1,128]{1,0:T(2,128)(2,1)} %bitcast.26, f32[1,128]{1,0:T(1,128)} %constant.15.clone.freq_hbm, s32[64,128]{1,0:T(8,128)} %bitcast.23, ...), custom_call_target="tpu_custom_call" | custom-call | flops 2147483648 | bytes 16777216 | tf_op jit(solution)/shard_map/prefill/pallas_call | solution.py:226
  16.4 15.3 %all_to_all.5.row_ref = bf16[16,80,128]{2,1,0:T(8,128)(2,1)S(1)} all-to-all(bf16[16,80,128]{2,1,0:T(8,128)(2,1)} %prefill.1), channel_id=1, replica_groups=mesh['role'=2,'batch'=8,'tensor'=8] {'role','batch'}, dimensions={0} | all-to-all | bytes 655360 | tf_op jit(solution)/shard_map/all_to_all | solution.py:448
  31.8 2.6 %attend.1 = bf16[8,64,128]{2,1,0:T(8,128)(2,1)S(1)} custom-call(s32[3]{0:T(128)S(1)} %copy-done.4, s32[256]{0:T(256)S(1)} %copy-done.5, s32[256]{0:T(256)S(1)} %copy-done.6, bf16[4,16,8,128]{3,2,1,0:T(8,128)(2,1)S(1)} %copy-done.2, bf16[16,512,128]{2,1,0:T(8,128)(2,1)S(1)} %bitcast.15, bf16[128,128]{1,0:T(8,128)(2,1)S(1)} %bitcast.17, ...), custom_call_target="tpu_custom_call" | custom-call | tf_op jit(solution)/shard_map/attend/pallas_call | solution.py:328
  34.4 0.7 collective-permute-start.3
  35.1 1.6 %collective-permute-start.2 = (bf16[8,64,128]{2,1,0:T(8,128)(2,1)S(1)}, bf16[8,64,128]{2,1,0:T(8,128)(2,1)S(1)}, u32[]{:S(2)}, u32[]{:S(2)}) collective-permute-start(bf16[8,64,128]{2,1,0:T(8,128)(2,1)S(1)} %attend.1), channel_id=1, source_target_pairs={{0,16},{8,24},{16,0},{24,8},{32,48},{40,56},{48,32},{56,40},{1,17}... | collective-permute-start | bytes 393224 | tf_op jit(solution)/shard_map/ppermute | solution.py:462
  36.7 1.9 %collective-permute-start.1 = (bf16[8,64,128]{2,1,0:T(8,128)(2,1)S(1)}, bf16[8,64,128]{2,1,0:T(8,128)(2,1)S(1)}, u32[]{:S(2)}, u32[]{:S(2)}) collective-permute-start(bf16[8,64,128]{2,1,0:T(8,128)(2,1)S(1)} %attend.1), channel_id=1, source_target_pairs={{0,8},{8,0},{16,24},{24,16},{32,40},{40,32},{48,56},{56,48},{1,9},... | collective-permute-start | bytes 393224 | tf_op jit(solution)/shard_map/ppermute | solution.py:462
  38.6 5.4 %collective-permute-done.3 = bf16[8,64,128]{2,1,0:T(8,128)(2,1)S(1)} collective-permute-done((bf16[8,64,128]{2,1,0:T(8,128)(2,1)S(1)}, bf16[8,64,128]{2,1,0:T(8,128)(2,1)S(1)}, u32[]{:S(2)}, u32[]{:S(2)}) %collective-permute-start.3) | collective-permute-done | bytes 131104 | tf_op jit(solution)/shard_map/ppermute | solution.py:462
  44.0 0.6 collective-permute-done.1
  44.7 0.1 collective-permute-start.4
  44.8 1.9 %collective-permute-done.4.other_ref = bf16[4,8,64,128]{3,2,1,0:T(8,128)(2,1)S(1)} collective-permute-done((bf16[4,8,64,128]{3,2,1,0:T(8,128)(2,1)S(1)}, bf16[4,8,64,128]{3,2,1,0:T(8,128)(2,1)S(1)}, u32[]{:S(2)}, u32[]{:S(2)}) %collective-permute-start.4) | collective-permute-done | bytes 524320 | tf_op jit(solution)/shard_map/ppermute | solution.py:464
  46.7 1.9 %project_out.1 = (bf16[128,512]{1,0:T(8,128)(2,1)S(1)}, bf16[128,512]{1,0:T(8,128)(2,1)S(1)}, bf16[128,512]{1,0:T(8,128)(2,1)S(1)}, bf16[128,512]{1,0:T(8,128)(2...) custom-call(s32[3]{0:T(128)S(1)} %copy-done.4, ...), custom_call_target="tpu_custom_call" | custom-call | tf_op jit(solution)/shard_map/project_out/pallas_call | solution.py:402
  48.5 0.7 collective-permute-start.5
  49.2 4.3 %collective-permute-start.6 = (bf16[128,512]{1,0:T(8,128)(2,1)S(1)}, bf16[128,512]{1,0:T(8,128)(2,1)S(1)}, u32[]{:S(2)}, u32[]{:S(2)}) collective-permute-start(bf16[128,512]{1,0:T(8,128)(2,1)S(1)} %get-tuple-element.18), channel_id=1, source_target_pairs={{0,32},{1,33},{2,0},{3,1},{4,36},{5,37},{6,4},{7,5},{8,40},{9,41},... | collective-permute-start | bytes 393224 | tf_op jit(solution)/shard_map/ppermute | solution.py:466
  53.6 3.0 %collective-permute-start.7 = (bf16[128,512]{1,0:T(8,128)(2,1)S(1)}, bf16[128,512]{1,0:T(8,128)(2,1)S(1)}, u32[]{:S(2)}, u32[]{:S(2)}) collective-permute-start(bf16[128,512]{1,0:T(8,128)(2,1)S(1)} %get-tuple-element.19), channel_id=1, source_target_pairs={{0,1},{1,0},{2,33},{3,32},{4,5},{5,4},{6,37},{7,36},{8,9},{9,8},{1... | collective-permute-start | bytes 393224 | tf_op jit(solution)/shard_map/ppermute | solution.py:466
  56.6 2.9 %collective-permute-start.9 = (bf16[128,512]{1,0:T(8,128)(2,1)S(1)}, bf16[128,512]{1,0:T(8,128)(2,1)S(1)}, u32[]{:S(2)}, u32[]{:S(2)}) collective-permute-start(bf16[128,512]{1,0:T(8,128)(2,1)S(1)} %get-tuple-element.21), channel_id=1, source_target_pairs={{0,4},{1,5},{2,36},{3,37},{4,0},{5,1},{6,32},{7,33},{8,12},{9,13},... | collective-permute-start | bytes 393224 | tf_op jit(solution)/shard_map/ppermute | solution.py:466
  59.5 3.3 %collective-permute-start.10 = (bf16[128,512]{1,0:T(8,128)(2,1)S(1)}, bf16[128,512]{1,0:T(8,128)(2,1)S(1)}, u32[]{:S(2)}, u32[]{:S(2)}) collective-permute-start(bf16[128,512]{1,0:T(8,128)(2,1)S(1)} %get-tuple-element.22), channel_id=1, source_target_pairs={{0,36},{1,37},{2,4},{3,5},{4,32},{5,33},{6,0},{7,1},{8,44},{9,45},... | collective-permute-start | bytes 393224 | tf_op jit(solution)/shard_map/ppermute | solution.py:466
  62.8 4.1 %collective-permute-start.11 = (bf16[128,512]{1,0:T(8,128)(2,1)S(1)}, bf16[128,512]{1,0:T(8,128)(2,1)S(1)}, u32[]{:S(2)}, u32[]{:S(2)}) collective-permute-start(bf16[128,512]{1,0:T(8,128)(2,1)S(1)} %get-tuple-element.23), channel_id=1, source_target_pairs={{0,5},{1,4},{2,37},{3,36},{4,1},{5,0},{6,33},{7,32},{8,13},{9,12},... | collective-permute-start | bytes 393224 | tf_op jit(solution)/shard_map/ppermute | solution.py:466
  66.9 0.9 %collective-permute-start.12 = (bf16[128,512]{1,0:T(8,128)(2,1)S(1)}, bf16[128,512]{1,0:T(8,128)(2,1)S(1)}, u32[]{:S(2)}, u32[]{:S(2)}) collective-permute-start(bf16[128,512]{1,0:T(8,128)(2,1)S(1)} %get-tuple-element.24), channel_id=1, source_target_pairs={{0,37},{1,36},{2,5},{3,4},{4,33},{5,32},{6,1},{7,0},{8,45},{9,44},... | collective-permute-start | bytes 393224 | tf_op jit(solution)/shard_map/ppermute | solution.py:466
  67.8 4.8 %collective-permute-done.11 = bf16[128,512]{1,0:T(8,128)(2,1)S(1)} collective-permute-done((bf16[128,512]{1,0:T(8,128)(2,1)S(1)}, bf16[128,512]{1,0:T(8,128)(2,1)S(1)}, u32[]{:S(2)}, u32[]{:S(2)}) %collective-permute-start.11) | collective-permute-done | bytes 131104 | tf_op jit(solution)/shard_map/ppermute | solution.py:466
  72.6 2.9 %collective-permute-done.12 = bf16[128,512]{1,0:T(8,128)(2,1)S(1)} collective-permute-done((bf16[128,512]{1,0:T(8,128)(2,1)S(1)}, bf16[128,512]{1,0:T(8,128)(2,1)S(1)}, u32[]{:S(2)}, u32[]{:S(2)}) %collective-permute-start.12) | collective-permute-done | bytes 131104 | tf_op jit(solution)/shard_map/ppermute | solution.py:466
  75.5 0.1 add_convert_fusion
  75.6 0.7 reshape.35
  (24 shorter events, 0.1 us)
Async XLA Ops:
  0.0 31.7 %collective-permute-start = (bf16[1024,512]{1,0:T(8,128)(2,1)}, bf16[1024,512]{1,0:T(8,128)(2,1)S(1)}, u32[]{:S(2)}, u32[]{:S(2)}) collective-permute-start(bf16[1024,512]{1,0:T(8,128)(2,1)} %own_ref.1), channel_id=1, source_target_pairs={{0,32},{8,40},{16,48},{24,56},{32,0},{40,8},{48,16},{56,24},{1,33}... | collective-permute-start | bytes 3145736 | tf_op jit(solution)/shard_map/ppermute | solution.py:436
  2.2 29.5 %copy-start = (bf16[16,256,1,2,128]{4,3,2,1,0:T(2,128)(2,1)S(1)}, bf16[16,256,1,2,128]{4,3,2,1,0:T(2,128)(2,1)}, u32[]{:S(2)}) copy-start(bf16[16,256,1,2,128]{4,3,2,1,0:T(2,128)(2,1)} %param.19) | copy-start | bytes 6291460
  2.2 29.5 %copy-start.2 = (bf16[4,16,8,128]{3,2,1,0:T(8,128)(2,1)S(1)}, bf16[4,16,8,128]{3,2,1,0:T(8,128)(2,1)}, u32[]{:S(2)}) copy-start(bf16[4,16,8,128]{3,2,1,0:T(8,128)(2,1)} %query_ref.1) | copy-start | bytes 393220
  2.2 29.5 %copy-start.3 = (bf16[4,16,1,2,128]{4,3,2,1,0:T(2,128)(2,1)S(1)}, bf16[4,16,1,2,128]{4,3,2,1,0:T(2,128)(2,1)}, u32[]{:S(2)}) copy-start(bf16[4,16,1,2,128]{4,3,2,1,0:T(2,128)(2,1)} %param.18) | copy-start | bytes 98308
  2.2 29.5 %copy-start.4 = (s32[3]{0:T(128)S(1)}, s32[3]{0:T(128)}, u32[]{:S(2)}) copy-start(s32[3]{0:T(128)} %pad_add_fusion.place) | copy-start | bytes 40
  2.2 29.5 %copy-start.5 = (s32[256]{0:T(256)S(1)}, s32[256]{0:T(256)}, u32[]{:S(2)}) copy-start(s32[256]{0:T(256)} %members.1) | copy-start | bytes 3076
  2.2 29.5 %copy-start.6 = (s32[256]{0:T(256)S(1)}, s32[256]{0:T(256)}, u32[]{:S(2)}) copy-start(s32[256]{0:T(256)} %cache_len.1) | copy-start | bytes 3076
  16.4 30.2 %copy-start.1 = (bf16[1024,512]{1,0:T(8,128)(2,1)S(1)}, bf16[1024,512]{1,0:T(8,128)(2,1)}, u32[]{:S(2)}) copy-start(bf16[1024,512]{1,0:T(8,128)(2,1)} %own_ref.1) | copy-start | bytes 3145732
  34.4 9.6 %collective-permute-start.3 = (bf16[8,64,128]{2,1,0:T(8,128)(2,1)S(1)}, bf16[8,64,128]{2,1,0:T(8,128)(2,1)S(1)}, u32[]{:S(2)}, u32[]{:S(2)}) collective-permute-start(bf16[8,64,128]{2,1,0:T(8,128)(2,1)S(1)} %attend.1), channel_id=1, source_target_pairs={{0,24},{8,16},{16,8},{24,0},{32,56},{40,48},{48,40},{56,32},{1,25}... | collective-permute-start | bytes 393224 | tf_op jit(solution)/shard_map/ppermute | solution.py:462
  35.1 8.9 %collective-permute-start.2 = (bf16[8,64,128]{2,1,0:T(8,128)(2,1)S(1)}, bf16[8,64,128]{2,1,0:T(8,128)(2,1)S(1)}, u32[]{:S(2)}, u32[]{:S(2)}) collective-permute-start(bf16[8,64,128]{2,1,0:T(8,128)(2,1)S(1)} %attend.1), channel_id=1, source_target_pairs={{0,16},{8,24},{16,0},{24,8},{32,48},{40,56},{48,32},{56,40},{1,17}... | collective-permute-start | bytes 393224 | tf_op jit(solution)/shard_map/ppermute | solution.py:462
  36.7 7.9 %collective-permute-start.1 = (bf16[8,64,128]{2,1,0:T(8,128)(2,1)S(1)}, bf16[8,64,128]{2,1,0:T(8,128)(2,1)S(1)}, u32[]{:S(2)}, u32[]{:S(2)}) collective-permute-start(bf16[8,64,128]{2,1,0:T(8,128)(2,1)S(1)} %attend.1), channel_id=1, source_target_pairs={{0,8},{8,0},{16,24},{24,16},{32,40},{40,32},{48,56},{56,48},{1,9},... | collective-permute-start | bytes 393224 | tf_op jit(solution)/shard_map/ppermute | solution.py:462
  44.7 2.0 %collective-permute-start.4 = (bf16[4,8,64,128]{3,2,1,0:T(8,128)(2,1)S(1)}, bf16[4,8,64,128]{3,2,1,0:T(8,128)(2,1)S(1)}, u32[]{:S(2)}, u32[]{:S(2)}) collective-permute-start(bf16[4,8,64,128]{3,2,1,0:T(8,128)(2,1)S(1)} %pad_maximum_fusion.mine_ref), channel_id=1, source_target_pairs={{0,64},{64,0},{1,65},{65,1},{2,66},{66,2},{3,67},{67,3},{4,68},{68... | collective-permute-start | bytes 1572872 | tf_op jit(solution)/shard_map/ppermute | solution.py:464
  48.5 11.0 %collective-permute-start.5 = (bf16[128,512]{1,0:T(8,128)(2,1)S(1)}, bf16[128,512]{1,0:T(8,128)(2,1)S(1)}, u32[]{:S(2)}, u32[]{:S(2)}) collective-permute-start(bf16[128,512]{1,0:T(8,128)(2,1)S(1)} %get-tuple-element.17), channel_id=1, source_target_pairs={{0,0},{1,1},{2,32},{3,33},{4,4},{5,5},{6,36},{7,37},{8,8},{9,9},{1... | collective-permute-start | bytes 393224 | tf_op jit(solution)/shard_map/ppermute | solution.py:466
  49.2 13.6 %collective-permute-start.6 = (bf16[128,512]{1,0:T(8,128)(2,1)S(1)}, bf16[128,512]{1,0:T(8,128)(2,1)S(1)}, u32[]{:S(2)}, u32[]{:S(2)}) collective-permute-start(bf16[128,512]{1,0:T(8,128)(2,1)S(1)} %get-tuple-element.18), channel_id=1, source_target_pairs={{0,32},{1,33},{2,0},{3,1},{4,36},{5,37},{6,4},{7,5},{8,40},{9,41},... | collective-permute-start | bytes 393224 | tf_op jit(solution)/shard_map/ppermute | solution.py:466
  53.6 13.3 %collective-permute-start.7 = (bf16[128,512]{1,0:T(8,128)(2,1)S(1)}, bf16[128,512]{1,0:T(8,128)(2,1)S(1)}, u32[]{:S(2)}, u32[]{:S(2)}) collective-permute-start(bf16[128,512]{1,0:T(8,128)(2,1)S(1)} %get-tuple-element.19), channel_id=1, source_target_pairs={{0,1},{1,0},{2,33},{3,32},{4,5},{5,4},{6,37},{7,36},{8,9},{9,8},{1... | collective-permute-start | bytes 393224 | tf_op jit(solution)/shard_map/ppermute | solution.py:466
  56.6 11.2 %collective-permute-start.8 = (bf16[128,512]{1,0:T(8,128)(2,1)S(1)}, bf16[128,512]{1,0:T(8,128)(2,1)S(1)}, u32[]{:S(2)}, u32[]{:S(2)}) collective-permute-start(bf16[128,512]{1,0:T(8,128)(2,1)S(1)} %get-tuple-element.20), channel_id=1, source_target_pairs={{0,33},{1,32},{2,1},{3,0},{4,37},{5,36},{6,5},{7,4},{8,41},{9,40},... | collective-permute-start | bytes 393224 | tf_op jit(solution)/shard_map/ppermute | solution.py:466
  56.6 11.2 %collective-permute-start.9 = (bf16[128,512]{1,0:T(8,128)(2,1)S(1)}, bf16[128,512]{1,0:T(8,128)(2,1)S(1)}, u32[]{:S(2)}, u32[]{:S(2)}) collective-permute-start(bf16[128,512]{1,0:T(8,128)(2,1)S(1)} %get-tuple-element.21), channel_id=1, source_target_pairs={{0,4},{1,5},{2,36},{3,37},{4,0},{5,1},{6,32},{7,33},{8,12},{9,13},... | collective-permute-start | bytes 393224 | tf_op jit(solution)/shard_map/ppermute | solution.py:466
  59.5 8.3 %collective-permute-start.10 = (bf16[128,512]{1,0:T(8,128)(2,1)S(1)}, bf16[128,512]{1,0:T(8,128)(2,1)S(1)}, u32[]{:S(2)}, u32[]{:S(2)}) collective-permute-start(bf16[128,512]{1,0:T(8,128)(2,1)S(1)} %get-tuple-element.22), channel_id=1, source_target_pairs={{0,36},{1,37},{2,4},{3,5},{4,32},{5,33},{6,0},{7,1},{8,44},{9,45},... | collective-permute-start | bytes 393224 | tf_op jit(solution)/shard_map/ppermute | solution.py:466
  62.8 9.9 %collective-permute-start.11 = (bf16[128,512]{1,0:T(8,128)(2,1)S(1)}, bf16[128,512]{1,0:T(8,128)(2,1)S(1)}, u32[]{:S(2)}, u32[]{:S(2)}) collective-permute-start(bf16[128,512]{1,0:T(8,128)(2,1)S(1)} %get-tuple-element.23), channel_id=1, source_target_pairs={{0,5},{1,4},{2,37},{3,36},{4,1},{5,0},{6,33},{7,32},{8,13},{9,12},... | collective-permute-start | bytes 393224 | tf_op jit(solution)/shard_map/ppermute | solution.py:466
  66.9 8.6 %collective-permute-start.12 = (bf16[128,512]{1,0:T(8,128)(2,1)S(1)}, bf16[128,512]{1,0:T(8,128)(2,1)S(1)}, u32[]{:S(2)}, u32[]{:S(2)}) collective-permute-start(bf16[128,512]{1,0:T(8,128)(2,1)S(1)} %get-tuple-element.24), channel_id=1, source_target_pairs={{0,37},{1,36},{2,5},{3,4},{4,33},{5,32},{6,1},{7,0},{8,45},{9,44},... | collective-permute-start | bytes 393224 | tf_op jit(solution)/shard_map/ppermute | solution.py:466

commit v4 on v3

--- a/solution.py
+++ b/solution.py
@@ -39,7 +39,6 @@
 
 
 def prefill_kernel(
-    place,
     x_hbm,
     weight_hbm,
     gain_hbm,
@@ -64,6 +63,7 @@
     weight_sem,
     small_sem,
 ):
+    role, batch = lax.axis_index("role"), lax.axis_index("batch")
     rows, width = x_hbm.shape
     depth = x_ref.shape[0]
     owners = out_ref.shape[0]
@@ -72,7 +72,7 @@
     slots = member_ref.shape[0] * 128
     per_owner = slots // owners
 
-    block = pl.ds(pl.multiple_of(place[1] * groups, 8), groups)
+    block = pl.ds(pl.multiple_of(batch * groups, 8), groups)
     small = [
         pltpu.make_async_copy(source, target, small_sem.at[index])
         for index, (source, target) in enumerate(
@@ -109,9 +109,16 @@
     members = member_ref[...]
     filler = jnp.zeros((8 - members.shape[0], 128), jnp.int32)
     turned = to_column(jnp.concatenate([members, filler], axis=0).astype(F32))
-    member_column = jnp.concatenate(
+    requests = request_ref[...].astype(F32)
+    held = jnp.concatenate(
         [
-            jnp.broadcast_to(turned[:, part : part + 1], (128, 128))
+            jnp.concatenate(
+                [
+                    as_mask(turned[:, part : part + 1] == requests[group : group + 1, :])
+                    for group in range(groups)
+                ],
+                axis=1,
+            )
             for part in range(slots // 128)
         ],
         axis=0,
@@ -120,24 +127,33 @@
     pick_slot = iota((32, slots), 1)
     pick = jnp.where(pick_row == owners, pick_slot % per_owner, 0)
     pick = jnp.where((pick_row < owners) & (pick_slot // per_owner == pick_row), 1, pick)
-    pick = pick.astype(F32).astype(BF16)
-    earlier = as_mask(iota((128, 128), 0) < iota((128, 128), 1))
-    ones = jnp.ones((128, 128), BF16)
-    carry = (iota((owners, 128), 0) * capacity).astype(F32)
-    ids = jnp.zeros((8, rows), F32)
-    for group in range(groups):
-        held = as_mask(member_column == request_ref[group : group + 1, :].astype(F32))
-        found = nn_dot(pick, held)
-        owner_hot = found[:owners]
-        hot = owner_hot.astype(BF16)
-        ranks = nn_dot(hot, earlier) + carry
-        carry = carry + nn_dot(hot, ones)
-        target = jnp.sum(owner_hot * ranks, axis=0, keepdims=True).astype(jnp.int32)
-        chosen = as_mask(iota((rows, 128), 0) == target)
-        perm_ref[group] = chosen
-        ids = ids + nt_dot(found[owners : owners + 8].astype(BF16), chosen)
-
-    positions = jnp.where(place[0] == 0, position_ref[...], 0)
+    found = nn_dot(pick.astype(F32).astype(BF16), held)
+    stack = jnp.concatenate(
+        [found[:owners, group * 128 : (group + 1) * 128] for group in range(groups)], axis=0
+    )
+    hot = stack.astype(BF16)
+    stacked = groups * owners
+    ranks = nn_dot(hot, as_mask(iota((128, 128), 0) < iota((128, 128), 1)))
+    totals = nn_dot(hot, jnp.ones((128, 128), BF16)).astype(BF16)
+    to_row, from_row = iota((stacked, stacked), 0), iota((stacked, stacked), 1)
+    prior = as_mask((from_row // owners < to_row // owners) & (from_row % owners == to_row % owners))
+    ranks = ranks + nn_dot(prior, totals)
+    ranks = ranks + ((iota((stacked, 128), 0) % owners) * capacity).astype(F32)
+    placed = stack * ranks
+    targets = [
+        jnp.sum(placed[group * owners : (group + 1) * owners], axis=0, keepdims=True).astype(
+            jnp.int32
+        )
+        for group in range(groups)
+    ]
+    slot_columns = to_column(
+        jnp.concatenate(
+            [found[owners : owners + 1, group * 128 : (group + 1) * 128] for group in range(groups)],
+            axis=0,
+        )
+    )
+
+    positions = jnp.where(role == 0, position_ref[...], 0)
     position_columns = 32.0 * to_column((positions >> 5).astype(F32)) + to_column(
         (positions & 31).astype(F32)
     )
@@ -192,21 +208,30 @@
         cosines = jnp.where(lane < 64, table, swapped)
         sines = jnp.where(lane < 64, -swapped, table)
         rotated = scaled * cosines + pltpu.roll(scaled, 64, axis=1) * sines
-        rounded_ref[group * 128 : (group + 1) * 128, :] = rotated.astype(BF16)
-
-    everything = jnp.concatenate([perm_ref[group] for group in range(groups)], axis=1)
-    ordered = nn_dot(everything, rounded_ref[...]).astype(BF16)
+        span = slice(group * 128, (group + 1) * 128)
+        rounded_ref[span, :128] = rotated.astype(BF16)
+        rounded_ref[span, 128:] = jnp.broadcast_to(
+            slot_columns[:, group : group + 1], (128, 128)
+        ).astype(BF16)
+        perm_ref[:, span] = as_mask(iota((rows, 128), 0) == targets[group])
+
+    ordered = nn_dot(perm_ref[...], rounded_ref[...])
+    diagonal = iota((128, 128), 0) == iota((128, 128), 1)
     lanes = iota((16, 128), 1)
     for owner in range(owners):
-        out_ref[owner, :capacity, :] = ordered[owner * capacity : (owner + 1) * capacity]
-        pair = owner // 2
-        both = jnp.broadcast_to(ids[0:1, pair * 128 : (pair + 1) * 128], (16, 128))
-        other = pltpu.roll(both, 64, axis=1)
+        span = slice(owner * capacity, (owner + 1) * capacity)
+        place = owner * 2 % owners + owner * 2 // owners
+        out_ref[place, :capacity, :] = ordered[span, :128].astype(BF16)
+        if owner % 2 == 0:
+            ids = ordered[owner * capacity : owner * capacity + 128, 128:]
+            ids = jnp.sum(jnp.where(diagonal, ids, 0.0), axis=0, keepdims=True)
+            both = jnp.broadcast_to(ids, (16, 128))
+            other = pltpu.roll(both, 64, axis=1)
         mine = (lanes < 64) if owner % 2 == 0 else (lanes >= 64)
-        out_ref[owner, capacity:, :] = jnp.where(mine, both, other).astype(BF16)
-
-
-def prefill(place, span_x, norm_gain, weight, bias, span_req, span_pos, members, owners):
+        out_ref[place, capacity:, :] = jnp.where(mine, both, other).astype(BF16)
+
+
+def prefill(span_x, norm_gain, weight, bias, span_req, span_pos, members, owners):
     rows, width = span_x.shape
     head_dim = weight.shape[1]
     groups = rows // 128
@@ -226,7 +251,7 @@
     return pl.pallas_call(
         prefill_kernel,
         out_shape=jax.ShapeDtypeStruct((owners, rows // owners + 16, head_dim), BF16),
-        in_specs=[pl.BlockSpec(memory_space=pltpu.SMEM)] + [pl.BlockSpec(memory_space=pl.ANY)] * 8,
+        in_specs=[pl.BlockSpec(memory_space=pl.ANY)] * 8,
         out_specs=pl.BlockSpec(memory_space=pltpu.VMEM),
         scratch_shapes=[
             pltpu.VMEM((depth, 128, width), BF16),
@@ -235,8 +260,8 @@
         + [pltpu.VMEM(shape, array.dtype) for shape, array in zip(held, small)]
         + [
             pltpu.VMEM((16, width), BF16),
-            pltpu.VMEM((groups, rows, 128), BF16),
-            pltpu.VMEM((rows, head_dim), BF16),
+            pltpu.VMEM((rows, rows), BF16),
+            pltpu.VMEM((rows, 2 * head_dim), BF16),
             pltpu.SemaphoreType.DMA((depth,)),
             pltpu.SemaphoreType.DMA,
             pltpu.SemaphoreType.DMA((len(small),)),
@@ -246,12 +271,13 @@
             flops=2 * rows * width * head_dim, bytes_accessed=2 * rows * width, transcendentals=0
         ),
         name="prefill",
-    )(place, span_x, weight, *small)
+    )(span_x, weight, *small)
 
 
 def attention_kernel(
-    place, members, cache_len, query_ref, cache_ref, fresh_ref, row_ref, out_ref, q_ref, s_ref, p_ref, sum_ref, acc_ref
+    members, cache_len, query_ref, cache_ref, fresh_ref, row_ref, out_ref, q_ref, s_ref, p_ref, sum_ref, acc_ref
 ):
+    place = (lax.axis_index("role"), lax.axis_index("batch"))
     steps, slots, heads, dim = query_ref.shape
     per_slot = steps * heads
     rows = slots * per_slot
@@ -273,14 +299,14 @@
         length = cache_len[members[owner * slots + slot]]
         keep = ((column & 1) == 0) & (column < 2 * length)
         s_ref[span, :cached] = jnp.where(keep, scores, NEGATIVE)
-    keys = [row_ref[block, :capacity, :] for block in range(blocks)]
-    values = [row_ref[blocks + block, :capacity, :] for block in range(blocks)]
+    keys = [row_ref[2 * block, :capacity, :] for block in range(blocks)]
+    values = [row_ref[2 * block + 1, :capacity, :] for block in range(blocks)]
     lane = iota((16, 128), 1)
     row_slot = iota((rows, 128), 0) // per_slot
     for pair in range(spanned // 128):
         scores = nt_dot(q_ref[...], jnp.concatenate(keys[2 * pair : 2 * pair + 2], axis=0)) * scale
-        left = row_ref[2 * pair, capacity:, :].astype(F32)
-        right = row_ref[2 * pair + 1, capacity:, :].astype(F32)
+        left = row_ref[4 * pair, capacity:, :].astype(F32)
+        right = row_ref[4 * pair + 2, capacity:, :].astype(F32)
         ids = jnp.where(lane < 64, left, right)[0:1].astype(jnp.int32)
         s_ref[:, cached + pair * 128 : cached + (pair + 1) * 128] = jnp.where(
             row_slot == ids, scores, NEGATIVE
@@ -318,7 +344,7 @@
         out_ref[head] = acc_ref[pl.ds(head, slots * steps, stride=heads), :].astype(BF16)
 
 
-def attend(place, members, cache_len, queries, cache, fresh, rows):
+def attend(members, cache_len, queries, cache, fresh, rows):
     steps, slots, heads, dim = queries.shape
     count = slots * steps * heads
     cached = cache.shape[1]
@@ -328,7 +354,7 @@
     return pl.pallas_call(
         attention_kernel,
         out_shape=jax.ShapeDtypeStruct((heads, slots * steps, dim), BF16),
-        in_specs=[pl.BlockSpec(memory_space=pltpu.SMEM)] * 3 + [vmem] * 4,
+        in_specs=[pl.BlockSpec(memory_space=pltpu.SMEM)] * 2 + [vmem] * 4,
         out_specs=vmem,
         scratch_shapes=[
             pltpu.VMEM((count, dim), BF16),
@@ -339,7 +365,7 @@
         ],
         compiler_params=pltpu.CompilerParams(vmem_limit_bytes=32 * MIB),
         name="attend",
-    )(place, members, cache_len, queries, cache, fresh, rows)
+    )(members, cache_len, queries, cache, fresh, rows)
 
 
 AXES = ("role", "batch", "tensor")
@@ -370,9 +396,9 @@
     )
 
 
-def project_kernel(place, mine_ref, other_ref, own_ref, x_ref, *rest):
+def project_kernel(mine_ref, other_ref, own_ref, x_ref, *rest):
     outs, staged = rest[:-1], rest[-1]
-    role, batch, tensor = place[0], place[1], place[2]
+    role, batch, tensor = (lax.axis_index(name) for name in AXES)
     x_lo, z_top, z_low = batch >> 2, (batch >> 1) & 1, batch & 1
     y, x_hi = tensor >> 1, tensor & 1
     blocks, heads, rows, _ = mine_ref.shape
@@ -395,19 +421,40 @@
         out[...] = staged[turn]
 
 
-def project_out(place, mine, other, *weights):
+def project_out(mine, other, *weights):
     _, heads, rows, _ = mine.shape
     columns = weights[0].shape[1]
     vmem = pl.BlockSpec(memory_space=pltpu.VMEM)
     return pl.pallas_call(
         project_kernel,
         out_shape=[jax.ShapeDtypeStruct((2 * rows, columns), BF16)] * 8,
-        in_specs=[pl.BlockSpec(memory_space=pltpu.SMEM)] + [vmem] * 4,
+        in_specs=[vmem] * 4,
         out_specs=[vmem] * 8,
         scratch_shapes=[pltpu.VMEM((8, 2 * rows, columns), BF16)],
         compiler_params=pltpu.CompilerParams(vmem_limit_bytes=32 * MIB),
         name="project_out",
-    )(place, mine, other, *weights)
+    )(mine, other, *weights)
+
+
+def add_kernel(*refs):
+    out_ref = refs[-1]
+    total = refs[0][...].astype(F32)
+    for ref in refs[1:-1]:
+        total = total + ref[...].astype(F32)
+    out_ref[...] = total.reshape(out_ref.shape).astype(BF16)
+
+
+def add_up(parts, steps):
+    rows, columns = parts[0].shape
+    vmem = pl.BlockSpec(memory_space=pltpu.VMEM)
+    return pl.pallas_call(
+        add_kernel,
+        out_shape=jax.ShapeDtypeStruct((rows // steps, steps, columns), BF16),
+        in_specs=[vmem] * len(parts),
+        out_specs=vmem,
+        compiler_params=pltpu.CompilerParams(vmem_limit_bytes=32 * MIB),
+        name="add_up",
+    )(*parts)
 
 
 def body(
@@ -427,15 +474,11 @@
     n_role = lax.axis_size("role")
     n_batch = lax.axis_size("batch")
     owners = n_role * n_batch
-    my_role = lax.axis_index("role")
-    my_batch = lax.axis_index("batch")
     width = span_x.shape[1]
     head_dim = key_value_weight.shape[3]
     steps, slots, heads, _ = queries.shape
-    place = jnp.stack([my_role, my_batch, lax.axis_index("tensor")]).astype(jnp.int32)
     beside = lax.ppermute(w_out, "batch", [(b, b ^ 4) for b in range(8)])
     outgoing = prefill(
-        place,
         span_x,
         norm_gain,
         key_value_weight.reshape(width, head_dim),
@@ -445,10 +488,9 @@
         members,
         owners,
     )
-    arrived = lax.all_to_all(outgoing, ("role", "batch"), 0, 0)
+    arrived = lax.all_to_all(outgoing, ("batch", "role"), 0, 0)
     arrived, beside = lax.optimization_barrier((arrived, beside))
     attention = attend(
-        place,
         members,
         cache_len,
         queries,
@@ -462,9 +504,8 @@
         + [lax.ppermute(attention, "batch", [(b, b ^ k) for b in range(8)]) for k in range(1, 4)]
     )
     other = lax.ppermute(gathered, "role", [(0, 1), (1, 0)])
-    parts = project_out(place, gathered, other, w_out, beside)
-    total = sum(lax.ppermute(parts[k], AXES, sum_round(k)).astype(F32) for k in range(8))
-    return total.astype(BF16).reshape(-1, steps, w_out.shape[1])
+    parts = project_out(gathered, other, w_out, beside)
+    return add_up([lax.ppermute(parts[k], AXES, sum_round(k)) for k in range(8)], steps)
 
 
 def solution(mesh):

time: 76.5 us -> 75.5 us (0.987)
  blocking collectives: 15.3 us -> 18.4 us
  Pallas kernels: 18.7 us -> 16.9 us
  waiting for transfers between devices: 15.5 us -> 14.7 us
  other arithmetic: 0.85 us -> 0.07 us
    all_to_all x1, blocking collectives: 15.3 us -> 18.4 us  [body(): arrived = lax.all_to_all(outgoing, ('batch', 'role'), 0, 0)]
    pallas_call x1, Pallas kernels: 14.2 us -> 12.2 us  [prefill(): pl.pallas_call(prefill_kernel, out_shape=jax.ShapeDtypeStruct((owners, ro...]
    ppermute x3, waiting for transfers between devices: 6 us -> 5.11 us  [body(): lax.ppermute(attention, 'batch', [(b, b ^ k) for b in range(8)])]
    pallas_call x0 -> x1, Pallas kernels: none -> 0.82 us  [add_up(): pl.pallas_call(add_kernel, out_shape=jax.ShapeDtypeStruct((rows // steps,...]
  transfers between devices with their start and end apart: 13 -> 13, of which waited for: 5 -> 5; matrix products, arithmetic and copies ran while one was open for 1% -> 0% of each run, Pallas kernels for 19% -> 16%
where the time goes in v4:
time: 75.5 us; the launch traced here: 75.3 us
  starting transfers between devices  25.1 us (33%)
  blocking collectives  18.4 us (24%)
  Pallas kernels  16.9 us (22%)
  waiting for transfers between devices  14.7 us (19%)
    ppermute x8, starting transfers between devices, body(): lax.ppermute(parts[k], AXES, sum_round(k))  19.3 us
    all_to_all x1, blocking collectives, body(): arrived = lax.all_to_all(outgoing, ('batch', 'role'), 0, 0)  18.4 us
    pallas_call x1, Pallas kernels, prefill(): pl.pallas_call(prefill_kernel, out_shape=jax.ShapeDtypeStruct((owners, ro...  12.2 us
    ppermute x8, waiting for transfers between devices, body(): lax.ppermute(parts[k], AXES, sum_round(k))  7.65 us
    ppermute x3, waiting for transfers between devices, body(): lax.ppermute(attention, 'batch', [(b, b ^ k) for b in range(8)])  5.11 us
    ppermute x3, starting transfers between devices, body(): lax.ppermute(attention, 'batch', [(b, b ^ k) for b in range(8)])  4.17 us
    pallas_call x1, Pallas kernels, attend(): pl.pallas_call(attention_kernel, out_shape=jax.ShapeDtypeStruct((heads, s...  2.62 us
    ppermute x1, waiting for transfers between devices, body(): other = lax.ppermute(gathered, 'role', [(0, 1), (1, 0)])  1.9 us
  transfers between devices with their start and end apart: 13, of which 5 were waited for; matrix products, arithmetic and copies ran while one was open for 0% of the time, Pallas kernels for 16%

profile of v4, /device:TPU:0, one launch (start us, length us, event | category | flops | bytes accessed | tf_op | source)
XLA Modules:
  0.0 75.3 jit_solution(112041285633571795)
XLA Ops:
  0.0 1.6 %collective-permute-start = (bf16[1024,512]{1,0:T(8,128)(2,1)}, bf16[1024,512]{1,0:T(8,128)(2,1)S(1)}, u32[]{:S(2)}, u32[]{:S(2)}) collective-permute-start(bf16[1024,512]{1,0:T(8,128)(2,1)} %own_ref.1), channel_id=1, source_target_pairs={{0,32},{8,40},{16,48},{24,56},{32,0},{40,8},{48,16},{56,24},{1,33}... | collective-permute-start | bytes 3145736 | tf_op jit(solution)/shard_map/ppermute | solution.py:480
  1.6 12.2 %prefill.1 = bf16[16,80,128]{2,1,0:T(8,128)(2,1)} custom-call(bf16[1024,8192]{1,0:T(8,128)(2,1)} %x_hbm.1, bf16[8192,128]{1,0:T(8,128)(2,1)} %bitcast.16, bf16[64,128]{1,0:T(8,128)(2,1)} %bitcast.22, bf16[1,128]{1,0:T(2,128)(2,1)} %bitcast.23, f32[1,128]{1,0:T(1,128)} %constant.2.clone.freq_hbm, s32[64,128]{1,0:T(8,128)} %bitcast.20, s32[64,128]{1,0:T(8,128)} %bitcast.21, ...), custom_call_target="tpu_custom_call" | custom-call | flops 2147483648 | bytes 16777216 | tf_op jit(solution)/shard_map/prefill/pallas_call | solution.py:251
  13.8 0.0 copy-start.1
  13.8 18.4 %all_to_all.5.row_ref = bf16[16,80,128]{2,1,0:T(8,128)(2,1)S(1)} all-to-all(bf16[16,80,128]{2,1,0:T(8,128)(2,1)} %prefill.1), channel_id=1, replica_groups=mesh['role'=2,'batch'=8,'tensor'=8] {'batch','role'}, dimensions={0} | all-to-all | bytes 655360 | tf_op jit(solution)/shard_map/all_to_all | solution.py:491
  32.2 2.6 %attend.1 = bf16[8,64,128]{2,1,0:T(8,128)(2,1)S(1)} custom-call(s32[256]{0:T(256)S(1)} %copy-done.4, s32[256]{0:T(256)S(1)} %copy-done.5, bf16[4,16,8,128]{3,2,1,0:T(8,128)(2,1)S(1)} %copy-done.2, bf16[16,512,128]{2,1,0:T(8,128)(2,1)S(1)} %bitcast.12, bf16[128,128]{1,0:T(8,128)(2,1)S(1)} %bitcast.14, bf16[16,80,128]{2,1,0:T(8,128)(2,1)S(1)} %all_to_all.5.row_ref), custom_call_target="tpu_custom_call" | custom-call | tf_op jit(solution)/shard_map/attend/pallas_call | solution.py:354
  34.8 0.1 collective-permute-start.3
  34.9 1.0 %collective-permute-start.2 = (bf16[8,64,128]{2,1,0:T(8,128)(2,1)S(1)}, bf16[8,64,128]{2,1,0:T(8,128)(2,1)S(1)}, u32[]{:S(2)}, u32[]{:S(2)}) collective-permute-start(bf16[8,64,128]{2,1,0:T(8,128)(2,1)S(1)} %attend.1), channel_id=1, source_target_pairs={{0,16},{8,24},{16,0},{24,8},{32,48},{40,56},{48,32},{56,40},{1,17}... | collective-permute-start | bytes 393224 | tf_op jit(solution)/shard_map/ppermute | solution.py:504
  35.9 3.1 %collective-permute-start.1 = (bf16[8,64,128]{2,1,0:T(8,128)(2,1)S(1)}, bf16[8,64,128]{2,1,0:T(8,128)(2,1)S(1)}, u32[]{:S(2)}, u32[]{:S(2)}) collective-permute-start(bf16[8,64,128]{2,1,0:T(8,128)(2,1)S(1)} %attend.1), channel_id=1, source_target_pairs={{0,8},{8,0},{16,24},{24,16},{32,40},{40,32},{48,56},{56,48},{1,9},... | collective-permute-start | bytes 393224 | tf_op jit(solution)/shard_map/ppermute | solution.py:504
  39.0 4.5 %collective-permute-done.3 = bf16[8,64,128]{2,1,0:T(8,128)(2,1)S(1)} collective-permute-done((bf16[8,64,128]{2,1,0:T(8,128)(2,1)S(1)}, bf16[8,64,128]{2,1,0:T(8,128)(2,1)S(1)}, u32[]{:S(2)}, u32[]{:S(2)}) %collective-permute-start.3) | collective-permute-done | bytes 131104 | tf_op jit(solution)/shard_map/ppermute | solution.py:504
  43.5 0.6 collective-permute-done.1
  44.1 0.1 pad_maximum_fusion.mine_ref
  44.2 0.1 collective-permute-start.4
  44.3 1.9 %collective-permute-done.4.other_ref = bf16[4,8,64,128]{3,2,1,0:T(8,128)(2,1)S(1)} collective-permute-done((bf16[4,8,64,128]{3,2,1,0:T(8,128)(2,1)S(1)}, bf16[4,8,64,128]{3,2,1,0:T(8,128)(2,1)S(1)}, u32[]{:S(2)}, u32[]{:S(2)}) %collective-permute-start.4) | collective-permute-done | bytes 524320 | tf_op jit(solution)/shard_map/ppermute | solution.py:506
  46.2 1.3 %project_out.1 = (bf16[128,512]{1,0:T(8,128)(2,1)S(1)}, bf16[128,512]{1,0:T(8,128)(2,1)S(1)}, bf16[128,512]{1,0:T(8,128)(2,1)S(1)}, bf16[128,512]{1,0:T(8,128)(2...) custom-call(bf16[4,8,64,128]{3,2,1,0:T(8,128)(2,1)S(1)} %pad_maximum, ...), custom_call_target="tpu_custom_call" | custom-call | tf_op jit(solution)/shard_map/project_out/pallas_call | solution.py:428
  47.5 0.7 collective-permute-start.5
  48.2 4.3 %collective-permute-start.6 = (bf16[128,512]{1,0:T(8,128)(2,1)S(1)}, bf16[128,512]{1,0:T(8,128)(2,1)S(1)}, u32[]{:S(2)}, u32[]{:S(2)}) collective-permute-start(bf16[128,512]{1,0:T(8,128)(2,1)S(1)} %get-tuple-element.18), channel_id=1, source_target_pairs={{0,32},{1,33},{2,0},{3,1},{4,36},{5,37},{6,4},{7,5},{8,40},{9,41},... | collective-permute-start | bytes 393224 | tf_op jit(solution)/shard_map/ppermute | solution.py:508
  52.5 3.0 %collective-permute-start.7 = (bf16[128,512]{1,0:T(8,128)(2,1)S(1)}, bf16[128,512]{1,0:T(8,128)(2,1)S(1)}, u32[]{:S(2)}, u32[]{:S(2)}) collective-permute-start(bf16[128,512]{1,0:T(8,128)(2,1)S(1)} %get-tuple-element.19), channel_id=1, source_target_pairs={{0,1},{1,0},{2,33},{3,32},{4,5},{5,4},{6,37},{7,36},{8,9},{9,8},{1... | collective-permute-start | bytes 393224 | tf_op jit(solution)/shard_map/ppermute | solution.py:508
  55.6 2.9 %collective-permute-start.9 = (bf16[128,512]{1,0:T(8,128)(2,1)S(1)}, bf16[128,512]{1,0:T(8,128)(2,1)S(1)}, u32[]{:S(2)}, u32[]{:S(2)}) collective-permute-start(bf16[128,512]{1,0:T(8,128)(2,1)S(1)} %get-tuple-element.21), channel_id=1, source_target_pairs={{0,4},{1,5},{2,36},{3,37},{4,0},{5,1},{6,32},{7,33},{8,12},{9,13},... | collective-permute-start | bytes 393224 | tf_op jit(solution)/shard_map/ppermute | solution.py:508
  58.5 3.2 %collective-permute-start.10 = (bf16[128,512]{1,0:T(8,128)(2,1)S(1)}, bf16[128,512]{1,0:T(8,128)(2,1)S(1)}, u32[]{:S(2)}, u32[]{:S(2)}) collective-permute-start(bf16[128,512]{1,0:T(8,128)(2,1)S(1)} %get-tuple-element.22), channel_id=1, source_target_pairs={{0,36},{1,37},{2,4},{3,5},{4,32},{5,33},{6,0},{7,1},{8,44},{9,45},... | collective-permute-start | bytes 393224 | tf_op jit(solution)/shard_map/ppermute | solution.py:508
  61.7 4.1 %collective-permute-start.11 = (bf16[128,512]{1,0:T(8,128)(2,1)S(1)}, bf16[128,512]{1,0:T(8,128)(2,1)S(1)}, u32[]{:S(2)}, u32[]{:S(2)}) collective-permute-start(bf16[128,512]{1,0:T(8,128)(2,1)S(1)} %get-tuple-element.23), channel_id=1, source_target_pairs={{0,5},{1,4},{2,37},{3,36},{4,1},{5,0},{6,33},{7,32},{8,13},{9,12},... | collective-permute-start | bytes 393224 | tf_op jit(solution)/shard_map/ppermute | solution.py:508
  65.9 0.9 %collective-permute-start.12 = (bf16[128,512]{1,0:T(8,128)(2,1)S(1)}, bf16[128,512]{1,0:T(8,128)(2,1)S(1)}, u32[]{:S(2)}, u32[]{:S(2)}) collective-permute-start(bf16[128,512]{1,0:T(8,128)(2,1)S(1)} %get-tuple-element.24), channel_id=1, source_target_pairs={{0,37},{1,36},{2,5},{3,4},{4,33},{5,32},{6,1},{7,0},{8,45},{9,44},... | collective-permute-start | bytes 393224 | tf_op jit(solution)/shard_map/ppermute | solution.py:508
  66.8 4.8 %collective-permute-done.11.refs_6_ = bf16[128,512]{1,0:T(8,128)(2,1)S(1)} collective-permute-done((bf16[128,512]{1,0:T(8,128)(2,1)S(1)}, bf16[128,512]{1,0:T(8,128)(2,1)S(1)}, u32[]{:S(2)}, u32[]{:S(2)}) %collective-permute-start.11) | collective-permute-done | bytes 131104 | tf_op jit(solution)/shard_map/ppermute | solution.py:508
  71.6 2.9 %collective-permute-done.12.refs_7_ = bf16[128,512]{1,0:T(8,128)(2,1)S(1)} collective-permute-done((bf16[128,512]{1,0:T(8,128)(2,1)S(1)}, bf16[128,512]{1,0:T(8,128)(2,1)S(1)}, u32[]{:S(2)}, u32[]{:S(2)}) %collective-permute-start.12) | collective-permute-done | bytes 131104 | tf_op jit(solution)/shard_map/ppermute | solution.py:508
  74.5 0.8 %add_up.1 = bf16[32,4,512]{2,1,0:T(4,128)(2,1)} custom-call(bf16[128,512]{1,0:T(8,128)(2,1)S(1)} %collective-permute-done.5.refs_0_, bf16[128,512]{1,0:T(8,128)(2,1)S(1)} %collective-permute-done.6.refs_1_, bf16[128,512]{1,0:T(8,128)(2,1)S(1)} %collective-permute-done.7.refs_2_, bf16[128,512]{1,0:T(8,128)(2,1)S(1)} %collective-permute-done.8.refs_3_, ...), custom_call_target="tpu_custom_call" | custom-call | tf_op jit(solution)/shard_map/add_up/pallas_call | solution.py:450
  (20 shorter events, 0.0 us)
Async XLA Ops:
  0.0 32.2 %collective-permute-start = (bf16[1024,512]{1,0:T(8,128)(2,1)}, bf16[1024,512]{1,0:T(8,128)(2,1)S(1)}, u32[]{:S(2)}, u32[]{:S(2)}) collective-permute-start(bf16[1024,512]{1,0:T(8,128)(2,1)} %own_ref.1), channel_id=1, source_target_pairs={{0,32},{8,40},{16,48},{24,56},{32,0},{40,8},{48,16},{56,24},{1,33}... | collective-permute-start | bytes 3145736 | tf_op jit(solution)/shard_map/ppermute | solution.py:480
  1.6 30.6 %copy-start = (bf16[16,256,1,2,128]{4,3,2,1,0:T(2,128)(2,1)S(1)}, bf16[16,256,1,2,128]{4,3,2,1,0:T(2,128)(2,1)}, u32[]{:S(2)}) copy-start(bf16[16,256,1,2,128]{4,3,2,1,0:T(2,128)(2,1)} %param.19) | copy-start | bytes 6291460
  1.6 30.6 %copy-start.2 = (bf16[4,16,8,128]{3,2,1,0:T(8,128)(2,1)S(1)}, bf16[4,16,8,128]{3,2,1,0:T(8,128)(2,1)}, u32[]{:S(2)}) copy-start(bf16[4,16,8,128]{3,2,1,0:T(8,128)(2,1)} %query_ref.1) | copy-start | bytes 393220
  1.6 30.6 %copy-start.3 = (bf16[4,16,1,2,128]{4,3,2,1,0:T(2,128)(2,1)S(1)}, bf16[4,16,1,2,128]{4,3,2,1,0:T(2,128)(2,1)}, u32[]{:S(2)}) copy-start(bf16[4,16,1,2,128]{4,3,2,1,0:T(2,128)(2,1)} %param.18) | copy-start | bytes 98308
  1.6 30.6 %copy-start.4 = (s32[256]{0:T(256)S(1)}, s32[256]{0:T(256)}, u32[]{:S(2)}) copy-start(s32[256]{0:T(256)} %members.1) | copy-start | bytes 3076
  1.6 30.6 %copy-start.5 = (s32[256]{0:T(256)S(1)}, s32[256]{0:T(256)}, u32[]{:S(2)}) copy-start(s32[256]{0:T(256)} %cache_len.1) | copy-start | bytes 3076
  13.8 32.4 %copy-start.1 = (bf16[1024,512]{1,0:T(8,128)(2,1)S(1)}, bf16[1024,512]{1,0:T(8,128)(2,1)}, u32[]{:S(2)}) copy-start(bf16[1024,512]{1,0:T(8,128)(2,1)} %own_ref.1) | copy-start | bytes 3145732
  34.8 8.7 %collective-permute-start.3 = (bf16[8,64,128]{2,1,0:T(8,128)(2,1)S(1)}, bf16[8,64,128]{2,1,0:T(8,128)(2,1)S(1)}, u32[]{:S(2)}, u32[]{:S(2)}) collective-permute-start(bf16[8,64,128]{2,1,0:T(8,128)(2,1)S(1)} %attend.1), channel_id=1, source_target_pairs={{0,24},{8,16},{16,8},{24,0},{32,56},{40,48},{48,40},{56,32},{1,25}... | collective-permute-start | bytes 393224 | tf_op jit(solution)/shard_map/ppermute | solution.py:504
  34.9 8.6 %collective-permute-start.2 = (bf16[8,64,128]{2,1,0:T(8,128)(2,1)S(1)}, bf16[8,64,128]{2,1,0:T(8,128)(2,1)S(1)}, u32[]{:S(2)}, u32[]{:S(2)}) collective-permute-start(bf16[8,64,128]{2,1,0:T(8,128)(2,1)S(1)} %attend.1), channel_id=1, source_target_pairs={{0,16},{8,24},{16,0},{24,8},{32,48},{40,56},{48,32},{56,40},{1,17}... | collective-permute-start | bytes 393224 | tf_op jit(solution)/shard_map/ppermute | solution.py:504
  35.9 8.2 %collective-permute-start.1 = (bf16[8,64,128]{2,1,0:T(8,128)(2,1)S(1)}, bf16[8,64,128]{2,1,0:T(8,128)(2,1)S(1)}, u32[]{:S(2)}, u32[]{:S(2)}) collective-permute-start(bf16[8,64,128]{2,1,0:T(8,128)(2,1)S(1)} %attend.1), channel_id=1, source_target_pairs={{0,8},{8,0},{16,24},{24,16},{32,40},{40,32},{48,56},{56,48},{1,9},... | collective-permute-start | bytes 393224 | tf_op jit(solution)/shard_map/ppermute | solution.py:504
  44.2 2.0 %collective-permute-start.4 = (bf16[4,8,64,128]{3,2,1,0:T(8,128)(2,1)S(1)}, bf16[4,8,64,128]{3,2,1,0:T(8,128)(2,1)S(1)}, u32[]{:S(2)}, u32[]{:S(2)}) collective-permute-start(bf16[4,8,64,128]{3,2,1,0:T(8,128)(2,1)S(1)} %pad_maximum_fusion.mine_ref), channel_id=1, source_target_pairs={{0,64},{64,0},{1,65},{65,1},{2,66},{66,2},{3,67},{67,3},{4,68},{68... | collective-permute-start | bytes 1572872 | tf_op jit(solution)/shard_map/ppermute | solution.py:506
  47.5 11.0 %collective-permute-start.5 = (bf16[128,512]{1,0:T(8,128)(2,1)S(1)}, bf16[128,512]{1,0:T(8,128)(2,1)S(1)}, u32[]{:S(2)}, u32[]{:S(2)}) collective-permute-start(bf16[128,512]{1,0:T(8,128)(2,1)S(1)} %get-tuple-element.17), channel_id=1, source_target_pairs={{0,0},{1,1},{2,32},{3,33},{4,4},{5,5},{6,36},{7,37},{8,8},{9,9},{1... | collective-permute-start | bytes 393224 | tf_op jit(solution)/shard_map/ppermute | solution.py:508
  48.2 13.5 %collective-permute-start.6 = (bf16[128,512]{1,0:T(8,128)(2,1)S(1)}, bf16[128,512]{1,0:T(8,128)(2,1)S(1)}, u32[]{:S(2)}, u32[]{:S(2)}) collective-permute-start(bf16[128,512]{1,0:T(8,128)(2,1)S(1)} %get-tuple-element.18), channel_id=1, source_target_pairs={{0,32},{1,33},{2,0},{3,1},{4,36},{5,37},{6,4},{7,5},{8,40},{9,41},... | collective-permute-start | bytes 393224 | tf_op jit(solution)/shard_map/ppermute | solution.py:508
  52.5 13.3 %collective-permute-start.7 = (bf16[128,512]{1,0:T(8,128)(2,1)S(1)}, bf16[128,512]{1,0:T(8,128)(2,1)S(1)}, u32[]{:S(2)}, u32[]{:S(2)}) collective-permute-start(bf16[128,512]{1,0:T(8,128)(2,1)S(1)} %get-tuple-element.19), channel_id=1, source_target_pairs={{0,1},{1,0},{2,33},{3,32},{4,5},{5,4},{6,37},{7,36},{8,9},{9,8},{1... | collective-permute-start | bytes 393224 | tf_op jit(solution)/shard_map/ppermute | solution.py:508
  55.6 11.3 %collective-permute-start.8 = (bf16[128,512]{1,0:T(8,128)(2,1)S(1)}, bf16[128,512]{1,0:T(8,128)(2,1)S(1)}, u32[]{:S(2)}, u32[]{:S(2)}) collective-permute-start(bf16[128,512]{1,0:T(8,128)(2,1)S(1)} %get-tuple-element.20), channel_id=1, source_target_pairs={{0,33},{1,32},{2,1},{3,0},{4,37},{5,36},{6,5},{7,4},{8,41},{9,40},... | collective-permute-start | bytes 393224 | tf_op jit(solution)/shard_map/ppermute | solution.py:508
  55.6 11.3 %collective-permute-start.9 = (bf16[128,512]{1,0:T(8,128)(2,1)S(1)}, bf16[128,512]{1,0:T(8,128)(2,1)S(1)}, u32[]{:S(2)}, u32[]{:S(2)}) collective-permute-start(bf16[128,512]{1,0:T(8,128)(2,1)S(1)} %get-tuple-element.21), channel_id=1, source_target_pairs={{0,4},{1,5},{2,36},{3,37},{4,0},{5,1},{6,32},{7,33},{8,12},{9,13},... | collective-permute-start | bytes 393224 | tf_op jit(solution)/shard_map/ppermute | solution.py:508
  58.5 8.3 %collective-permute-start.10 = (bf16[128,512]{1,0:T(8,128)(2,1)S(1)}, bf16[128,512]{1,0:T(8,128)(2,1)S(1)}, u32[]{:S(2)}, u32[]{:S(2)}) collective-permute-start(bf16[128,512]{1,0:T(8,128)(2,1)S(1)} %get-tuple-element.22), channel_id=1, source_target_pairs={{0,36},{1,37},{2,4},{3,5},{4,32},{5,33},{6,0},{7,1},{8,44},{9,45},... | collective-permute-start | bytes 393224 | tf_op jit(solution)/shard_map/ppermute | solution.py:508
  61.7 9.9 %collective-permute-start.11 = (bf16[128,512]{1,0:T(8,128)(2,1)S(1)}, bf16[128,512]{1,0:T(8,128)(2,1)S(1)}, u32[]{:S(2)}, u32[]{:S(2)}) collective-permute-start(bf16[128,512]{1,0:T(8,128)(2,1)S(1)} %get-tuple-element.23), channel_id=1, source_target_pairs={{0,5},{1,4},{2,37},{3,36},{4,1},{5,0},{6,33},{7,32},{8,13},{9,12},... | collective-permute-start | bytes 393224 | tf_op jit(solution)/shard_map/ppermute | solution.py:508
  65.9 8.6 %collective-permute-start.12 = (bf16[128,512]{1,0:T(8,128)(2,1)S(1)}, bf16[128,512]{1,0:T(8,128)(2,1)S(1)}, u32[]{:S(2)}, u32[]{:S(2)}) collective-permute-start(bf16[128,512]{1,0:T(8,128)(2,1)S(1)} %get-tuple-element.24), channel_id=1, source_target_pairs={{0,37},{1,36},{2,5},{3,4},{4,33},{5,32},{6,1},{7,0},{8,45},{9,44},... | collective-permute-start | bytes 393224 | tf_op jit(solution)/shard_map/ppermute | solution.py:508

commit v5 on v4

--- a/solution.py
+++ b/solution.py
@@ -505,7 +505,8 @@
     )
     other = lax.ppermute(gathered, "role", [(0, 1), (1, 0)])
     parts = project_out(gathered, other, w_out, beside)
-    return add_up([lax.ppermute(parts[k], AXES, sum_round(k)) for k in range(8)], steps)
+    order = (0, 1, 3, 2, 6, 7, 5, 4)
+    return add_up([lax.ppermute(parts[k], AXES, sum_round(k)) for k in order], steps)
 
 
 def solution(mesh):

time: 75.5 us -> 77 us (1.020); the launches traced: 75.3 us -> 75.9 us
  waiting for transfers between devices: 14.7 us -> 16.6 us
  starting transfers between devices: 25.1 us -> 23.8 us
    ppermute x8, waiting for transfers between devices: 7.65 us -> 9.55 us  [body(): lax.ppermute(parts[k], AXES, sum_round(k))]
    ppermute x8, starting transfers between devices: 19.3 us -> 18 us  [body(): lax.ppermute(parts[k], AXES, sum_round(k))]
  transfers between devices with their start and end apart: 13 -> 13, of which waited for: 5 -> 6; matrix products, arithmetic and copies ran while one was open for 0% -> 0% of each run, Pallas kernels for 16% -> 16%
where the time goes in v5:
time: 77 us; the launch traced here: 75.9 us
  starting transfers between devices  23.8 us (31%)
  blocking collectives  18.4 us (24%)
  Pallas kernels  16.9 us (22%)
  waiting for transfers between devices  16.6 us (22%)
    all_to_all x1, blocking collectives, body(): arrived = lax.all_to_all(outgoing, ('batch', 'role'), 0, 0)  18.4 us
    ppermute x8, starting transfers between devices, body(): lax.ppermute(parts[k], AXES, sum_round(k))  18 us
    pallas_call x1, Pallas kernels, prefill(): pl.pallas_call(prefill_kernel, out_shape=jax.ShapeDtypeStruct((owners, ro...  12.2 us
    ppermute x8, waiting for transfers between devices, body(): lax.ppermute(parts[k], AXES, sum_round(k))  9.55 us
    ppermute x3, waiting for transfers between devices, body(): lax.ppermute(attention, 'batch', [(b, b ^ k) for b in range(8)])  5.11 us
    ppermute x3, starting transfers between devices, body(): lax.ppermute(attention, 'batch', [(b, b ^ k) for b in range(8)])  4.17 us
    pallas_call x1, Pallas kernels, attend(): pl.pallas_call(attention_kernel, out_shape=jax.ShapeDtypeStruct((heads, s...  2.62 us
    ppermute x1, waiting for transfers between devices, body(): other = lax.ppermute(gathered, 'role', [(0, 1), (1, 0)])  1.9 us
  transfers between devices with their start and end apart: 13, of which 6 were waited for; matrix products, arithmetic and copies ran while one was open for 0% of the time, Pallas kernels for 16%

profile of v5, /device:TPU:0, one launch (start us, length us, event | category | flops | bytes accessed | tf_op | source)
XLA Modules:
  0.0 75.9 jit_solution(9991440629311541656)
XLA Ops:
  0.0 1.6 %collective-permute-start = (bf16[1024,512]{1,0:T(8,128)(2,1)}, bf16[1024,512]{1,0:T(8,128)(2,1)S(1)}, u32[]{:S(2)}, u32[]{:S(2)}) collective-permute-start(bf16[1024,512]{1,0:T(8,128)(2,1)} %own_ref.1), channel_id=1, source_target_pairs={{0,32},{8,40},{16,48},{24,56},{32,0},{40,8},{48,16},{56,24},{1,33}... | collective-permute-start | bytes 3145736 | tf_op jit(solution)/shard_map/ppermute | solution.py:480
  1.6 12.2 %prefill.1 = bf16[16,80,128]{2,1,0:T(8,128)(2,1)} custom-call(bf16[1024,8192]{1,0:T(8,128)(2,1)} %x_hbm.1, bf16[8192,128]{1,0:T(8,128)(2,1)} %bitcast.16, bf16[64,128]{1,0:T(8,128)(2,1)} %bitcast.22, bf16[1,128]{1,0:T(2,128)(2,1)} %bitcast.23, f32[1,128]{1,0:T(1,128)} %constant.2.clone.freq_hbm, s32[64,128]{1,0:T(8,128)} %bitcast.20, s32[64,128]{1,0:T(8,128)} %bitcast.21, ...), custom_call_target="tpu_custom_call" | custom-call | flops 2147483648 | bytes 16777216 | tf_op jit(solution)/shard_map/prefill/pallas_call | solution.py:251
  13.8 18.4 %all_to_all.5.row_ref = bf16[16,80,128]{2,1,0:T(8,128)(2,1)S(1)} all-to-all(bf16[16,80,128]{2,1,0:T(8,128)(2,1)} %prefill.1), channel_id=1, replica_groups=mesh['role'=2,'batch'=8,'tensor'=8] {'batch','role'}, dimensions={0} | all-to-all | bytes 655360 | tf_op jit(solution)/shard_map/all_to_all | solution.py:491
  32.2 2.6 %attend.1 = bf16[8,64,128]{2,1,0:T(8,128)(2,1)S(1)} custom-call(s32[256]{0:T(256)S(1)} %copy-done.4, s32[256]{0:T(256)S(1)} %copy-done.5, bf16[4,16,8,128]{3,2,1,0:T(8,128)(2,1)S(1)} %copy-done.2, bf16[16,512,128]{2,1,0:T(8,128)(2,1)S(1)} %bitcast.12, bf16[128,128]{1,0:T(8,128)(2,1)S(1)} %bitcast.14, bf16[16,80,128]{2,1,0:T(8,128)(2,1)S(1)} %all_to_all.5.row_ref), custom_call_target="tpu_custom_call" | custom-call | tf_op jit(solution)/shard_map/attend/pallas_call | solution.py:354
  34.8 0.1 collective-permute-start.3
  34.9 1.0 %collective-permute-start.2 = (bf16[8,64,128]{2,1,0:T(8,128)(2,1)S(1)}, bf16[8,64,128]{2,1,0:T(8,128)(2,1)S(1)}, u32[]{:S(2)}, u32[]{:S(2)}) collective-permute-start(bf16[8,64,128]{2,1,0:T(8,128)(2,1)S(1)} %attend.1), channel_id=1, source_target_pairs={{0,16},{8,24},{16,0},{24,8},{32,48},{40,56},{48,32},{56,40},{1,17}... | collective-permute-start | bytes 393224 | tf_op jit(solution)/shard_map/ppermute | solution.py:504
  35.9 3.1 %collective-permute-start.1 = (bf16[8,64,128]{2,1,0:T(8,128)(2,1)S(1)}, bf16[8,64,128]{2,1,0:T(8,128)(2,1)S(1)}, u32[]{:S(2)}, u32[]{:S(2)}) collective-permute-start(bf16[8,64,128]{2,1,0:T(8,128)(2,1)S(1)} %attend.1), channel_id=1, source_target_pairs={{0,8},{8,0},{16,24},{24,16},{32,40},{40,32},{48,56},{56,48},{1,9},... | collective-permute-start | bytes 393224 | tf_op jit(solution)/shard_map/ppermute | solution.py:504
  39.0 4.5 %collective-permute-done.3 = bf16[8,64,128]{2,1,0:T(8,128)(2,1)S(1)} collective-permute-done((bf16[8,64,128]{2,1,0:T(8,128)(2,1)S(1)}, bf16[8,64,128]{2,1,0:T(8,128)(2,1)S(1)}, u32[]{:S(2)}, u32[]{:S(2)}) %collective-permute-start.3) | collective-permute-done | bytes 131104 | tf_op jit(solution)/shard_map/ppermute | solution.py:504
  43.5 0.6 collective-permute-done.1
  44.2 0.1 collective-permute-start.4
  44.3 1.9 %collective-permute-done.4.other_ref = bf16[4,8,64,128]{3,2,1,0:T(8,128)(2,1)S(1)} collective-permute-done((bf16[4,8,64,128]{3,2,1,0:T(8,128)(2,1)S(1)}, bf16[4,8,64,128]{3,2,1,0:T(8,128)(2,1)S(1)}, u32[]{:S(2)}, u32[]{:S(2)}) %collective-permute-start.4) | collective-permute-done | bytes 524320 | tf_op jit(solution)/shard_map/ppermute | solution.py:506
  46.2 1.3 %project_out.1 = (bf16[128,512]{1,0:T(8,128)(2,1)S(1)}, bf16[128,512]{1,0:T(8,128)(2,1)S(1)}, bf16[128,512]{1,0:T(8,128)(2,1)S(1)}, bf16[128,512]{1,0:T(8,128)(2...) custom-call(bf16[4,8,64,128]{3,2,1,0:T(8,128)(2,1)S(1)} %pad_maximum, ...), custom_call_target="tpu_custom_call" | custom-call | tf_op jit(solution)/shard_map/project_out/pallas_call | solution.py:428
  47.5 0.7 collective-permute-start.5
  48.2 4.3 %collective-permute-start.6 = (bf16[128,512]{1,0:T(8,128)(2,1)S(1)}, bf16[128,512]{1,0:T(8,128)(2,1)S(1)}, u32[]{:S(2)}, u32[]{:S(2)}) collective-permute-start(bf16[128,512]{1,0:T(8,128)(2,1)S(1)} %get-tuple-element.18), channel_id=1, source_target_pairs={{0,32},{1,33},{2,0},{3,1},{4,36},{5,37},{6,4},{7,5},{8,40},{9,41},... | collective-permute-start | bytes 393224 | tf_op jit(solution)/shard_map/ppermute | solution.py:509
  52.5 1.6 %collective-permute-start.7 = (bf16[128,512]{1,0:T(8,128)(2,1)S(1)}, bf16[128,512]{1,0:T(8,128)(2,1)S(1)}, u32[]{:S(2)}, u32[]{:S(2)}) collective-permute-start(bf16[128,512]{1,0:T(8,128)(2,1)S(1)} %get-tuple-element.19), channel_id=1, source_target_pairs={{0,33},{1,32},{2,1},{3,0},{4,37},{5,36},{6,5},{7,4},{8,41},{9,40},... | collective-permute-start | bytes 393224 | tf_op jit(solution)/shard_map/ppermute | solution.py:509
  54.2 1.4 %collective-permute-start.8 = (bf16[128,512]{1,0:T(8,128)(2,1)S(1)}, bf16[128,512]{1,0:T(8,128)(2,1)S(1)}, u32[]{:S(2)}, u32[]{:S(2)}) collective-permute-start(bf16[128,512]{1,0:T(8,128)(2,1)S(1)} %get-tuple-element.20), channel_id=1, source_target_pairs={{0,1},{1,0},{2,33},{3,32},{4,5},{5,4},{6,37},{7,36},{8,9},{9,8},{1... | collective-permute-start | bytes 393224 | tf_op jit(solution)/shard_map/ppermute | solution.py:509
  55.6 4.5 %collective-permute-start.9 = (bf16[128,512]{1,0:T(8,128)(2,1)S(1)}, bf16[128,512]{1,0:T(8,128)(2,1)S(1)}, u32[]{:S(2)}, u32[]{:S(2)}) collective-permute-start(bf16[128,512]{1,0:T(8,128)(2,1)S(1)} %get-tuple-element.21), channel_id=1, source_target_pairs={{0,5},{1,4},{2,37},{3,36},{4,1},{5,0},{6,33},{7,32},{8,13},{9,12},... | collective-permute-start | bytes 393224 | tf_op jit(solution)/shard_map/ppermute | solution.py:509
  60.1 2.2 %collective-permute-start.10 = (bf16[128,512]{1,0:T(8,128)(2,1)S(1)}, bf16[128,512]{1,0:T(8,128)(2,1)S(1)}, u32[]{:S(2)}, u32[]{:S(2)}) collective-permute-start(bf16[128,512]{1,0:T(8,128)(2,1)S(1)} %get-tuple-element.22), channel_id=1, source_target_pairs={{0,37},{1,36},{2,5},{3,4},{4,33},{5,32},{6,1},{7,0},{8,45},{9,44},... | collective-permute-start | bytes 393224 | tf_op jit(solution)/shard_map/ppermute | solution.py:509
  62.2 0.9 %collective-permute-start.11 = (bf16[128,512]{1,0:T(8,128)(2,1)S(1)}, bf16[128,512]{1,0:T(8,128)(2,1)S(1)}, u32[]{:S(2)}, u32[]{:S(2)}) collective-permute-start(bf16[128,512]{1,0:T(8,128)(2,1)S(1)} %get-tuple-element.23), channel_id=1, source_target_pairs={{0,36},{1,37},{2,4},{3,5},{4,32},{5,33},{6,0},{7,1},{8,44},{9,45},... | collective-permute-start | bytes 393224 | tf_op jit(solution)/shard_map/ppermute | solution.py:509
  63.1 2.4 %collective-permute-start.12 = (bf16[128,512]{1,0:T(8,128)(2,1)S(1)}, bf16[128,512]{1,0:T(8,128)(2,1)S(1)}, u32[]{:S(2)}, u32[]{:S(2)}) collective-permute-start(bf16[128,512]{1,0:T(8,128)(2,1)S(1)} %get-tuple-element.24), channel_id=1, source_target_pairs={{0,4},{1,5},{2,36},{3,37},{4,0},{5,1},{6,32},{7,33},{8,12},{9,13},... | collective-permute-start | bytes 393224 | tf_op jit(solution)/shard_map/ppermute | solution.py:509
  65.5 3.2 %collective-permute-done.9.refs_4_ = bf16[128,512]{1,0:T(8,128)(2,1)S(1)} collective-permute-done((bf16[128,512]{1,0:T(8,128)(2,1)S(1)}, bf16[128,512]{1,0:T(8,128)(2,1)S(1)}, u32[]{:S(2)}, u32[]{:S(2)}) %collective-permute-start.9) | collective-permute-done | bytes 131104 | tf_op jit(solution)/shard_map/ppermute | solution.py:509
  68.8 1.1 %collective-permute-done.10.refs_5_ = bf16[128,512]{1,0:T(8,128)(2,1)S(1)} collective-permute-done((bf16[128,512]{1,0:T(8,128)(2,1)S(1)}, bf16[128,512]{1,0:T(8,128)(2,1)S(1)}, u32[]{:S(2)}, u32[]{:S(2)}) %collective-permute-start.10) | collective-permute-done | bytes 131104 | tf_op jit(solution)/shard_map/ppermute | solution.py:509
  69.9 5.2 %collective-permute-done.11.refs_6_ = bf16[128,512]{1,0:T(8,128)(2,1)S(1)} collective-permute-done((bf16[128,512]{1,0:T(8,128)(2,1)S(1)}, bf16[128,512]{1,0:T(8,128)(2,1)S(1)}, u32[]{:S(2)}, u32[]{:S(2)}) %collective-permute-start.11) | collective-permute-done | bytes 131104 | tf_op jit(solution)/shard_map/ppermute | solution.py:509
  75.1 0.8 %add_up.1 = bf16[32,4,512]{2,1,0:T(4,128)(2,1)} custom-call(bf16[128,512]{1,0:T(8,128)(2,1)S(1)} %collective-permute-done.5.refs_0_, bf16[128,512]{1,0:T(8,128)(2,1)S(1)} %collective-permute-done.6.refs_1_, bf16[128,512]{1,0:T(8,128)(2,1)S(1)} %collective-permute-done.7.refs_2_, bf16[128,512]{1,0:T(8,128)(2,1)S(1)} %collective-permute-done.8.refs_3_, ...), custom_call_target="tpu_custom_call" | custom-call | tf_op jit(solution)/shard_map/add_up/pallas_call | solution.py:450
  (20 shorter events, 0.1 us)
Async XLA Ops:
  0.0 32.2 %collective-permute-start = (bf16[1024,512]{1,0:T(8,128)(2,1)}, bf16[1024,512]{1,0:T(8,128)(2,1)S(1)}, u32[]{:S(2)}, u32[]{:S(2)}) collective-permute-start(bf16[1024,512]{1,0:T(8,128)(2,1)} %own_ref.1), channel_id=1, source_target_pairs={{0,32},{8,40},{16,48},{24,56},{32,0},{40,8},{48,16},{56,24},{1,33}... | collective-permute-start | bytes 3145736 | tf_op jit(solution)/shard_map/ppermute | solution.py:480
  1.6 30.6 %copy-start = (bf16[16,256,1,2,128]{4,3,2,1,0:T(2,128)(2,1)S(1)}, bf16[16,256,1,2,128]{4,3,2,1,0:T(2,128)(2,1)}, u32[]{:S(2)}) copy-start(bf16[16,256,1,2,128]{4,3,2,1,0:T(2,128)(2,1)} %param.19) | copy-start | bytes 6291460
  1.6 30.6 %copy-start.2 = (bf16[4,16,8,128]{3,2,1,0:T(8,128)(2,1)S(1)}, bf16[4,16,8,128]{3,2,1,0:T(8,128)(2,1)}, u32[]{:S(2)}) copy-start(bf16[4,16,8,128]{3,2,1,0:T(8,128)(2,1)} %query_ref.1) | copy-start | bytes 393220
  1.6 30.6 %copy-start.3 = (bf16[4,16,1,2,128]{4,3,2,1,0:T(2,128)(2,1)S(1)}, bf16[4,16,1,2,128]{4,3,2,1,0:T(2,128)(2,1)}, u32[]{:S(2)}) copy-start(bf16[4,16,1,2,128]{4,3,2,1,0:T(2,128)(2,1)} %param.18) | copy-start | bytes 98308
  1.6 30.6 %copy-start.4 = (s32[256]{0:T(256)S(1)}, s32[256]{0:T(256)}, u32[]{:S(2)}) copy-start(s32[256]{0:T(256)} %members.1) | copy-start | bytes 3076
  1.6 30.6 %copy-start.5 = (s32[256]{0:T(256)S(1)}, s32[256]{0:T(256)}, u32[]{:S(2)}) copy-start(s32[256]{0:T(256)} %cache_len.1) | copy-start | bytes 3076
  13.8 32.4 %copy-start.1 = (bf16[1024,512]{1,0:T(8,128)(2,1)S(1)}, bf16[1024,512]{1,0:T(8,128)(2,1)}, u32[]{:S(2)}) copy-start(bf16[1024,512]{1,0:T(8,128)(2,1)} %own_ref.1) | copy-start | bytes 3145732
  34.8 8.7 %collective-permute-start.3 = (bf16[8,64,128]{2,1,0:T(8,128)(2,1)S(1)}, bf16[8,64,128]{2,1,0:T(8,128)(2,1)S(1)}, u32[]{:S(2)}, u32[]{:S(2)}) collective-permute-start(bf16[8,64,128]{2,1,0:T(8,128)(2,1)S(1)} %attend.1), channel_id=1, source_target_pairs={{0,24},{8,16},{16,8},{24,0},{32,56},{40,48},{48,40},{56,32},{1,25}... | collective-permute-start | bytes 393224 | tf_op jit(solution)/shard_map/ppermute | solution.py:504
  34.9 8.6 %collective-permute-start.2 = (bf16[8,64,128]{2,1,0:T(8,128)(2,1)S(1)}, bf16[8,64,128]{2,1,0:T(8,128)(2,1)S(1)}, u32[]{:S(2)}, u32[]{:S(2)}) collective-permute-start(bf16[8,64,128]{2,1,0:T(8,128)(2,1)S(1)} %attend.1), channel_id=1, source_target_pairs={{0,16},{8,24},{16,0},{24,8},{32,48},{40,56},{48,32},{56,40},{1,17}... | collective-permute-start | bytes 393224 | tf_op jit(solution)/shard_map/ppermute | solution.py:504
  35.9 8.2 %collective-permute-start.1 = (bf16[8,64,128]{2,1,0:T(8,128)(2,1)S(1)}, bf16[8,64,128]{2,1,0:T(8,128)(2,1)S(1)}, u32[]{:S(2)}, u32[]{:S(2)}) collective-permute-start(bf16[8,64,128]{2,1,0:T(8,128)(2,1)S(1)} %attend.1), channel_id=1, source_target_pairs={{0,8},{8,0},{16,24},{24,16},{32,40},{40,32},{48,56},{56,48},{1,9},... | collective-permute-start | bytes 393224 | tf_op jit(solution)/shard_map/ppermute | solution.py:504
  44.2 2.0 %collective-permute-start.4 = (bf16[4,8,64,128]{3,2,1,0:T(8,128)(2,1)S(1)}, bf16[4,8,64,128]{3,2,1,0:T(8,128)(2,1)S(1)}, u32[]{:S(2)}, u32[]{:S(2)}) collective-permute-start(bf16[4,8,64,128]{3,2,1,0:T(8,128)(2,1)S(1)} %pad_maximum_fusion.mine_ref), channel_id=1, source_target_pairs={{0,64},{64,0},{1,65},{65,1},{2,66},{66,2},{3,67},{67,3},{4,68},{68... | collective-permute-start | bytes 1572872 | tf_op jit(solution)/shard_map/ppermute | solution.py:506
  47.5 12.5 %collective-permute-start.5 = (bf16[128,512]{1,0:T(8,128)(2,1)S(1)}, bf16[128,512]{1,0:T(8,128)(2,1)S(1)}, u32[]{:S(2)}, u32[]{:S(2)}) collective-permute-start(bf16[128,512]{1,0:T(8,128)(2,1)S(1)} %get-tuple-element.17), channel_id=1, source_target_pairs={{0,0},{1,1},{2,32},{3,33},{4,4},{5,5},{6,36},{7,37},{8,8},{9,9},{1... | collective-permute-start | bytes 393224 | tf_op jit(solution)/shard_map/ppermute | solution.py:509
  48.2 14.0 %collective-permute-start.6 = (bf16[128,512]{1,0:T(8,128)(2,1)S(1)}, bf16[128,512]{1,0:T(8,128)(2,1)S(1)}, u32[]{:S(2)}, u32[]{:S(2)}) collective-permute-start(bf16[128,512]{1,0:T(8,128)(2,1)S(1)} %get-tuple-element.18), channel_id=1, source_target_pairs={{0,32},{1,33},{2,0},{3,1},{4,36},{5,37},{6,4},{7,5},{8,40},{9,41},... | collective-permute-start | bytes 393224 | tf_op jit(solution)/shard_map/ppermute | solution.py:509
  52.5 10.6 %collective-permute-start.7 = (bf16[128,512]{1,0:T(8,128)(2,1)S(1)}, bf16[128,512]{1,0:T(8,128)(2,1)S(1)}, u32[]{:S(2)}, u32[]{:S(2)}) collective-permute-start(bf16[128,512]{1,0:T(8,128)(2,1)S(1)} %get-tuple-element.19), channel_id=1, source_target_pairs={{0,33},{1,32},{2,1},{3,0},{4,37},{5,36},{6,5},{7,4},{8,41},{9,40},... | collective-permute-start | bytes 393224 | tf_op jit(solution)/shard_map/ppermute | solution.py:509
  54.2 11.3 %collective-permute-start.8 = (bf16[128,512]{1,0:T(8,128)(2,1)S(1)}, bf16[128,512]{1,0:T(8,128)(2,1)S(1)}, u32[]{:S(2)}, u32[]{:S(2)}) collective-permute-start(bf16[128,512]{1,0:T(8,128)(2,1)S(1)} %get-tuple-element.20), channel_id=1, source_target_pairs={{0,1},{1,0},{2,33},{3,32},{4,5},{5,4},{6,37},{7,36},{8,9},{9,8},{1... | collective-permute-start | bytes 393224 | tf_op jit(solution)/shard_map/ppermute | solution.py:509
  55.6 13.2 %collective-permute-start.9 = (bf16[128,512]{1,0:T(8,128)(2,1)S(1)}, bf16[128,512]{1,0:T(8,128)(2,1)S(1)}, u32[]{:S(2)}, u32[]{:S(2)}) collective-permute-start(bf16[128,512]{1,0:T(8,128)(2,1)S(1)} %get-tuple-element.21), channel_id=1, source_target_pairs={{0,5},{1,4},{2,37},{3,36},{4,1},{5,0},{6,33},{7,32},{8,13},{9,12},... | collective-permute-start | bytes 393224 | tf_op jit(solution)/shard_map/ppermute | solution.py:509
  60.1 9.8 %collective-permute-start.10 = (bf16[128,512]{1,0:T(8,128)(2,1)S(1)}, bf16[128,512]{1,0:T(8,128)(2,1)S(1)}, u32[]{:S(2)}, u32[]{:S(2)}) collective-permute-start(bf16[128,512]{1,0:T(8,128)(2,1)S(1)} %get-tuple-element.22), channel_id=1, source_target_pairs={{0,37},{1,36},{2,5},{3,4},{4,33},{5,32},{6,1},{7,0},{8,45},{9,44},... | collective-permute-start | bytes 393224 | tf_op jit(solution)/shard_map/ppermute | solution.py:509
  62.2 12.8 %collective-permute-start.11 = (bf16[128,512]{1,0:T(8,128)(2,1)S(1)}, bf16[128,512]{1,0:T(8,128)(2,1)S(1)}, u32[]{:S(2)}, u32[]{:S(2)}) collective-permute-start(bf16[128,512]{1,0:T(8,128)(2,1)S(1)} %get-tuple-element.23), channel_id=1, source_target_pairs={{0,36},{1,37},{2,4},{3,5},{4,32},{5,33},{6,0},{7,1},{8,44},{9,45},... | collective-permute-start | bytes 393224 | tf_op jit(solution)/shard_map/ppermute | solution.py:509
  63.1 11.9 %collective-permute-start.12 = (bf16[128,512]{1,0:T(8,128)(2,1)S(1)}, bf16[128,512]{1,0:T(8,128)(2,1)S(1)}, u32[]{:S(2)}, u32[]{:S(2)}) collective-permute-start(bf16[128,512]{1,0:T(8,128)(2,1)S(1)} %get-tuple-element.24), channel_id=1, source_target_pairs={{0,4},{1,5},{2,36},{3,37},{4,0},{5,1},{6,32},{7,33},{8,12},{9,13},... | collective-permute-start | bytes 393224 | tf_op jit(solution)/shard_map/ppermute | solution.py:509
